TPU v7x, 32 devices: a whole 2x2x4 slice. The times are simulated.
32 devices in a mesh: region: 8 (over z, x), chan: 4 (over y, core).
Axes of the slice: x: 2, y: 2, z: 4, core: 2. Of those that a mesh axis runs over, the one named last changes fastest.
Arguments:
- point_feats: bfloat16 [64, 131072], P('chan', 'region'), may hold values from -6 to 6
- destination: int32 [131072], P('region'), may hold values from 0 to 7, as said below
- voxel_slot: int32 [131072], P('region'), may hold values from 0 to 32767, as said below
- adjacency: int32 [512, 26], P('region'), may hold values from 0 to 512, as said below
- active_count: int32 [8], P('region'), may hold values from 4 to 64, as said below
- conv_weight: bfloat16 [64, 64, 3, 3, 3], P('chan'), may hold values from -0.15625 to 0.15625
- down_weight: bfloat16 [128, 64, 2, 2, 2], P(None, 'chan'), may hold values from -0.25 to 0.25
Outputs:
- coarse: bfloat16 [512, 8192], P('region', 'chan')
Inputs may be any that keep to these rules, and one draw needn't show every extreme that they name: `destination`: each block of 16384 consecutive points names every region exactly 16384 / 8 times. Every point lies in an active brick of its region: voxel_slot // 512 < active_count[destination]. `adjacency`: entry n of row g names the brick at offset n from g, or 512 where that brick is inactive or off the map; rows of inactive slots hold only 512; the relation is symmetric. A neighbour at dx = 0 lies in g's own region, one at dx = -1 in that region or the previous one, one at dx = +1 in that region or the next one. In every region at most 16 active bricks have a neighbour in the next region and at most 16 in the previous one, and some region reaches 16 for each side. A region's active bricks fill its slots 0 to active_count - 1; some region fills all 64.
All inputs are finite; a program needn't handle non-finite values.
Results may differ from a plain program's by a relative error of at most 0.0053.
Values may be sent and summed in bfloat16 or wider, within the bound.
No kernel may reach another device: no remote copies, remote signals or barrier semaphores. Data moves between devices by JAX's collectives and lax.ppermute only.
A program may use at most 128 MiB of HBM per device.

v0:
```python
import functools

import jax
import jax.numpy as jnp
import numpy as np
from jax import lax
from jax.experimental import pallas as pl
from jax.experimental.pallas import tpu as pltpu
from jax.sharding import PartitionSpec as P

OFFSETS = [
    (first, second, third)
    for first in (-1, 0, 1)
    for second in (-1, 0, 1)
    for third in (-1, 0, 1)
    if (first, second, third) != (0, 0, 0)
]
LANES = 128
REACH = 16
F32 = jnp.float32
BF16 = jnp.bfloat16
NT = (((1,), (1,)), ((), ()))
VMEM = pl.BlockSpec(memory_space=pltpu.VMEM)
SMEM = pl.BlockSpec(memory_space=pltpu.SMEM)


def mm(a, b):
    return jnp.dot(a, b, preferred_element_type=F32)


def params():
    return pltpu.CompilerParams(vmem_limit_bytes=24 * 1024 * 1024)


ID_ROWS = 16
GROUP = 8


def one_hot_columns(depth, stack, wanted, channels=16):
    count = wanted.shape[0]
    width = count * LANES
    wanted = jnp.concatenate([wanted[i : i + 1] for i in range(count)], axis=1)
    low = (wanted & (depth - 1)).astype(jnp.int16)
    top = wanted // depth
    hot = lax.broadcasted_iota(jnp.int16, (depth, width), 0) == low
    hot = jnp.where(hot, jnp.ones((), BF16), jnp.zeros((), BF16))
    found = mm(stack[...], hot)
    picked = jnp.zeros((channels, width), F32)
    for part in range(stack.shape[0] // channels):
        picked = jnp.where(top == part, found[part * channels : (part + 1) * channels], picked)
    return picked.astype(BF16)


def fill_stack(depth, feats, stack):
    channels, points = feats.shape
    for part in range(points // depth):
        stack[part * channels : (part + 1) * channels, :] = feats[:, part * depth : (part + 1) * depth]


def put_codes(out, blocks, tiles, tile, rows):
    if rows.shape[0] < ID_ROWS:
        rows = jnp.concatenate([rows, jnp.zeros((ID_ROWS - rows.shape[0], LANES), jnp.int32)], axis=0)
    out[blocks + tile] = (rows >> 8).astype(F32).astype(BF16)
    out[blocks + tiles + tile] = (rows & 255).astype(F32).astype(BF16)


def permute_kernel(depth, width, cells, feats, order, keys, out, stack):
    channels, points = feats.shape
    fill_stack(depth, feats, stack)
    regions = out.shape[0]
    blocks = points // regions // LANES
    tiles = (out.shape[1] - blocks) // 2
    count = width // LANES

    def step(at, _):
        picked = one_hot_columns(depth, stack, order[pl.ds(at * count, count), :])
        for part in range(count):
            tile = at * count + part
            out[tile // blocks, tile % blocks] = picked[:, part * LANES : (part + 1) * LANES]
        return 0

    lax.fori_loop(0, points // width, step, 0)
    for target in range(regions):
        for tile in range(tiles):
            begin = target * blocks + tile * ID_ROWS
            rows = min(ID_ROWS, blocks - tile * ID_ROWS)
            put_codes(out.at[target], blocks, tiles, tile, lax.rem(keys[begin : begin + rows, :], cells))


def permute(feats, order, keys, regions, cells):
    channels, points = feats.shape
    depth, width = 512, 1024
    blocks = points // regions // LANES
    tiles = -(-blocks // ID_ROWS)
    return pl.pallas_call(
        functools.partial(permute_kernel, depth, width, cells),
        out_shape=jax.ShapeDtypeStruct((regions, blocks + 2 * tiles, channels, LANES), BF16),
        in_specs=[VMEM] * 3,
        out_specs=VMEM,
        scratch_shapes=[pltpu.VMEM((points // depth * channels, depth), BF16)],
        compiler_params=params(),
        name="permute",
    )(feats, order, keys)


def rotated(rows):
    before = jnp.concatenate([rows[-1:], rows[:-1]], axis=0)
    return jnp.concatenate([before[:, LANES // 2 :], rows[:, : LANES // 2]], axis=1)


def piece_kernel(depth, cells, flips, region, feats, order, keys, *rest):
    outs = rest[-1 - len(flips) : -1]
    stack = rest[-1]
    fill_stack(depth, feats, stack)
    tiles = 1
    blocks = outs[0].shape[0] - 2 * tiles
    count = 8
    for flip, out in zip(flips, outs):
        begin = pl.multiple_of((region[0] ^ flip) * blocks, 8)
        wanted = rotated(order[pl.ds(begin, blocks), :])
        for step in range(blocks // count):
            picked = one_hot_columns(depth, stack, wanted[step * count : (step + 1) * count])
            for part in range(count):
                out[step * count + part] = picked[:, part * LANES : (part + 1) * LANES]
        put_codes(out, blocks, tiles, 0, rotated(lax.rem(keys[pl.ds(begin, blocks), :], cells)))


def permute_piece(flips, region, feats, order, keys, regions, cells, before=()):
    channels, points = feats.shape
    depth = 512
    blocks = points // regions // LANES
    return pl.pallas_call(
        functools.partial(piece_kernel, depth, cells, flips),
        out_shape=[jax.ShapeDtypeStruct((blocks + 2, channels, LANES), BF16)] * len(flips),
        in_specs=[SMEM] + [VMEM] * 3 + [pl.BlockSpec(memory_space=pl.ANY)] * len(before),
        out_specs=[VMEM] * len(flips),
        scratch_shapes=[pltpu.VMEM((points // depth * channels, depth), BF16)],
        compiler_params=params(),
        cost_estimate=pl.CostEstimate(flops=2_000_000_000, bytes_accessed=1_000_000, transcendentals=0),
        name="permute_piece",
    )(region, feats, order, keys, *before)


def exchange(feats, order, keys, region, regions, cells):
    blocks = feats.shape[1] // regions // LANES
    if regions != GROUP or blocks != ID_ROWS:
        moved = permute(feats, order, keys, regions, cells)
        return [lax.all_to_all(moved, "region", 0, 0, tiled=True)], moved

    def send(values, flips):
        pairs = [[(source, source ^ flip) for source in range(regions)] for flip in flips]
        return [lax.ppermute(value, "region", pair) for value, pair in zip(values, pairs)]

    at = region.reshape(1)
    made = []
    got = []
    for number, flips in enumerate(((6, 7), (4, 5), (2, 3, 1, 0))):
        before = [*got[number - 2], made[-1][0]] if number >= 2 else ()
        values = permute_piece(flips, at, feats, order, keys, regions, cells, before)
        made.append(values)
        sent = sum(flip != 0 for flip in flips)
        got.append(send(values[:sent], flips[:sent]) + list(values[sent:]))
    return [chunk for some in got for chunk in some], made[2][0]


WINDOW = 256


def chunk_of(chunks, number):
    return chunks[0].at[number] if len(chunks) == 1 else chunks[number]


def decode(chunks, ids, ends, places):
    count, padded_blocks, _ = ids.shape
    tiles = padded_blocks // ID_ROWS
    blocks = chunk_of(chunks, 0).shape[0] - 2 * tiles
    bounds = lax.broadcasted_iota(jnp.int32, (ID_ROWS, LANES), 1) * (WINDOW * 8)
    row = lax.broadcasted_iota(jnp.int32, (ID_ROWS, LANES), 0)
    for chunk in range(count):
        first = jnp.zeros((1, LANES), jnp.int32)
        last = jnp.zeros((1, LANES), jnp.int32)
        for tile in range(tiles):
            upper = chunk_of(chunks, chunk)[blocks + tile].astype(F32)
            lower = chunk_of(chunks, chunk)[blocks + tiles + tile].astype(F32)
            code = (upper * 256.0 + lower).astype(jnp.int32)
            ids[chunk, tile * ID_ROWS : (tile + 1) * ID_ROWS, :] = code
            real = row + tile * ID_ROWS < blocks
            passed = real & (code[:, LANES - 1 :] < bounds)
            head = code[:, 0:1]
            if len(chunks) > 1:
                last += jnp.where(head[0:1] < bounds[0:1] + WINDOW * 8, 1, 0)
                head = jnp.where(row[:, 0:1] == 0, code[:, LANES // 2 : LANES // 2 + 1], head)
            begun = real & (head < bounds + WINDOW * 8)
            first += jnp.sum(jnp.where(passed, 1, 0), axis=0, keepdims=True)
            last += jnp.sum(jnp.where(begun, 1, 0), axis=0, keepdims=True)
        ends[chunk : chunk + 1, :] = first
        ends[count + chunk : count + chunk + 1, :] = last
    pltpu.sync_copy(ends, places)


def window_mean(number, chunks, ids, places, acc):
    count, padded_blocks, _ = ids.shape
    channels = chunk_of(chunks, 0).shape[1]
    groups = count // GROUP
    blocks = chunk_of(chunks, 0).shape[0] - 2 * (padded_blocks // ID_ROWS)

    lane = lax.broadcasted_iota(jnp.int32, (1, LANES), 1)

    def product(group, steps, static=False):
        sides = []
        rows = []
        for at in steps:
            for member in range(GROUP):
                chunk = group * GROUP + member
                if static:
                    block = number + at
                else:
                    block = places[chunk, number] + at
                    valid = block < places[count + chunk, number]
                if len(chunks) == 1:
                    block = jnp.minimum(block, blocks - 1)
                else:
                    begin = jnp.where(block == 0, LANES // 2, 0)
                    end = jnp.where(block == blocks, LANES // 2, LANES)
                    if not static:
                        end = jnp.where(valid & ((block < number) | (block > number + 1)), end, 0)
                    valid = (lane >= begin) & (lane < end)
                    block = block & (blocks - 1)
                code = ids[chunk, pl.ds(block, 1), :]
                cell = code & 7
                rows.append(jnp.where(valid, (code >> 3) - number * WINDOW, -1))
                values = chunk_of(chunks, chunk)[block].astype(F32)
                mask = [cell == k for k in range(8)]
                side = [jnp.where(m, values, 0.0).astype(BF16) for m in mask]
                side += [jnp.broadcast_to(jnp.where(m, 1.0, 0.0), (channels, LANES)).astype(BF16) for m in mask]
                sides.append(jnp.concatenate(side, axis=0))
        side = jnp.concatenate(sides, axis=1)
        row = jnp.concatenate(rows, axis=1).astype(jnp.int16)
        hot = lax.broadcasted_iota(jnp.int16, (WINDOW, len(steps) * GROUP * LANES), 0) == row
        hot = jnp.where(hot, jnp.ones((), BF16), jnp.zeros((), BF16))
        return lax.dot_general(hot, side, NT, preferred_element_type=F32)

    def one_group(group, start):
        def step(at, _):
            acc[...] += product(group, [at])
            return 0

        hops = 0
        for member in range(GROUP):
            chunk = group * GROUP + member
            first, last = places[chunk, number], places[count + chunk, number]
            need = last - first
            if len(chunks) > 1:
                need = jnp.where((first < number) | (last > number + 2), need, 0)
            hops = jnp.maximum(hops, need)
        lax.fori_loop(start, hops, step, 0)

    if len(chunks) > 1:
        acc[...] = product(0, [0, 1], static=True)
        one_group(0, 0)
    else:
        acc[...] = jnp.zeros_like(acc)

        def each(group, _):
            one_group(group, 0)
            return 0

        lax.fori_loop(0, groups, each, 0)
    return (acc[:, :LANES] / jnp.maximum(acc[:, LANES:], 1.0)).astype(BF16)


def far_kernel(count, chan, *rest):
    chunks = rest[:count]
    out, ids, acc, ends, places = rest[-5:]
    decode(chunks, ids, ends, places)
    begin = 2 * (chan[0] ^ 2) + 7
    parts = out.shape[1] // WINDOW
    for plane in range(out.shape[0]):
        for part in range(parts):
            number = lax.rem(begin + plane, 8) * parts + part
            out[plane, part * WINDOW : (part + 1) * WINDOW, :] = window_mean(number, chunks, ids, places, acc)


def near_kernel(slots, count, chan, *rest):
    chunks = rest[:count]
    far, send_pos, three, one, own, f0, f1, f2, f3, ids, acc, ends, places, planes = rest[count:]
    decode(chunks, ids, ends, places)
    partner = chan[0] ^ 2
    begin = 2 * partner + 7
    parts = far.shape[1] // WINDOW
    planes[0:4] = far[...]
    for plane in range(4, 8):
        for part in range(parts):
            number = lax.rem(begin + plane, 8) * parts + part
            planes[plane, part * WINDOW : (part + 1) * WINDOW, :] = window_mean(number, chunks, ids, places, acc)
    for out, flip in ((three, 3), (one, 1), (own, 0)):
        shift = 2 * ((chan[0] ^ flip) - partner) + 8
        if flip == 3:
            shift = shift + 2 * ((chan[0] ^ 3) & 1)
        for plane in range(out.shape[0]):
            out[plane] = planes[lax.rem(shift + plane, 8)]
    compact = []
    for side in range(2):
        hot = lax.broadcasted_iota(jnp.int32, (REACH, slots), 0) == send_pos[side : side + 1, :]
        compact.append(jnp.where(hot, 1.0, 0.0).astype(BF16))
    last_plane, first_plane = (planes.at[lax.rem(at - begin + 16, 8)] for at in (7, 8))
    for j in range(8):
        rows = slice(j * slots, (j + 1) * slots)
        to_next = mm(compact[0], last_plane[rows, :])
        to_previous = mm(compact[1], first_plane[rows, :])
        for flip, out in enumerate((f0, f1, f2, f3)):
            out[j] = jnp.where(chan[0] == flip, to_next, to_previous).astype(BF16)


def voxel_scratch(chunks, regions):
    total = chunks[0].shape[-3]
    tiles = -(-total // (ID_ROWS + 2))
    return [
        pltpu.VMEM((regions, tiles * ID_ROWS, LANES), jnp.int32),
        pltpu.VMEM((WINDOW, 2 * LANES), F32),
        pltpu.VMEM((2 * regions, LANES), jnp.int32),
        pltpu.SMEM((2 * regions, LANES), jnp.int32),
    ]


def far_voxels(chan, chunks, regions, slots, before):
    return pl.pallas_call(
        functools.partial(far_kernel, len(chunks)),
        out_shape=jax.ShapeDtypeStruct((4, 8 * slots, LANES), BF16),
        in_specs=[SMEM] + [VMEM] * len(chunks) + [pl.BlockSpec(memory_space=pl.ANY)] * len(before),
        out_specs=VMEM,
        scratch_shapes=voxel_scratch(chunks, regions),
        compiler_params=params(),
        cost_estimate=pl.CostEstimate(flops=4_000_000_000, bytes_accessed=1_200_000, transcendentals=0),
        name="far_voxels",
    )(chan, *chunks, *before)


def near_voxels(chan, chunks, regions, far, send_pos, slots):
    return pl.pallas_call(
        functools.partial(near_kernel, slots, len(chunks)),
        out_shape=[jax.ShapeDtypeStruct((planes, 8 * slots, LANES), BF16) for planes in (2, 4, 4)]
        + [jax.ShapeDtypeStruct((8, REACH, LANES), BF16)] * 4,
        in_specs=[SMEM] + [VMEM] * len(chunks) + [VMEM, VMEM],
        out_specs=[VMEM] * 7,
        scratch_shapes=voxel_scratch(chunks, regions) + [pltpu.VMEM((8, 8 * slots, LANES), BF16)],
        compiler_params=params(),
        cost_estimate=pl.CostEstimate(flops=4_000_000_000, bytes_accessed=3_000_000, transcendentals=0),
        name="near_voxels",
    )(chan, *chunks, far, send_pos)


def shared_kernel(chan, planes, out):
    begin = 2 - 2 * (chan[0] & 1)
    for plane in range(2):
        out[plane] = planes[begin + plane]


def shared_planes(chan, planes):
    return pl.pallas_call(
        shared_kernel,
        out_shape=jax.ShapeDtypeStruct((2, *planes.shape[1:]), BF16),
        in_specs=[SMEM, VMEM],
        out_specs=VMEM,
        compiler_params=pltpu.CompilerParams(vmem_limit_bytes=4 * 1024 * 1024),
        name="shared_planes",
    )(chan, planes)


def pack_kernel(conv, down, _, pack):
    for ab in range(9):
        for e in range(3):
            pack[ab, :, e * 64 : (e + 1) * 64] = conv[ab * 3 + e]
    for part in range(8):
        pack[9 + part, :, 0:128] = down[part * 16 : (part + 1) * 16, :]
        pack[9 + part, :, 128:192] = jnp.zeros((16, 64), BF16)


def pack(conv, down, before):
    return pl.pallas_call(
        pack_kernel,
        out_shape=jax.ShapeDtypeStruct((17, 16, 192), BF16),
        in_specs=[VMEM, VMEM, pl.BlockSpec(memory_space=pl.ANY)],
        out_specs=VMEM,
        compiler_params=params(),
        name="pack",
    )(conv, down, before)


def weight_kernel(chan, own, one, two, three, even, odd, down):
    every = (own, one, two, three)
    columns = lax.broadcasted_iota(jnp.int32, (192, 192), 1) ^ (chan[0] * 16)
    turn = jnp.where(lax.broadcasted_iota(jnp.int32, (192, 192), 0) == columns, 1.0, 0.0).astype(BF16)
    for out in (even, odd):
        out[...] = jnp.zeros_like(out)
    for ab in range(9):
        taps = jnp.concatenate([ref[ab] for ref in every], axis=0)
        turned = lax.dot_general(turn, taps, NT, preferred_element_type=F32)
        turned = jnp.concatenate([turned, turned], axis=1).astype(BF16)
        for e in range(3):
            for source in range(4):
                out, place = (even, odd)[source % 2], source // 2
                rows = turned[e * 64 + source * 16 : e * 64 + source * 16 + 16]
                for k in range(4):
                    piece = rows[:, (k % 2) * 64 : (k % 2) * 64 + 64]
                    column = slice(k * 64, (k + 1) * 64)
                    cell = k + e
                    if 1 <= cell <= 4:
                        row = place * 64 + (cell - 1) * 16
                        out[0, ab, row : row + 16, column] = piece
                        out[1, ab, 128 + row : 144 + row, column] = piece
                    else:
                        row = (cell // 5) * 32 + place * 16
                        out[0, ab, 128 + row : 144 + row, column] = piece
                        out[1, ab, 64 + row : 80 + row, column] = piece
    outputs = down.shape[0]
    total = jnp.zeros((outputs, 512), F32)
    rows = lax.broadcasted_iota(jnp.int32, (128, 512), 0)
    place = (rows & 7) * 64 + (rows >> 3)
    for source, ref in enumerate(every):
        part = ref[9:, :, 0:128].reshape(128, outputs)
        move = lax.broadcasted_iota(jnp.int32, (128, 512), 1) == place + source * 16
        move = jnp.where(move, 1.0, 0.0).astype(BF16)
        total += lax.dot_general(part, move, (((0,), (0,)), ((), ())), preferred_element_type=F32)
    down[...] = total.astype(BF16)


def prepare(chan, own, others, outputs):
    return pl.pallas_call(
        weight_kernel,
        out_shape=(
            jax.ShapeDtypeStruct((2, 9, 256, 256), BF16),
            jax.ShapeDtypeStruct((2, 9, 256, 256), BF16),
            jax.ShapeDtypeStruct((outputs, 512), BF16),
        ),
        in_specs=[SMEM] + [VMEM] * 4,
        out_specs=(VMEM, VMEM, VMEM),
        compiler_params=params(),
        cost_estimate=pl.CostEstimate(flops=2_000_000_000, bytes_accessed=3_000_000, transcendentals=0),
        name="prepare",
    )(chan, own, *others)


def halo_matrix():
    pick = np.zeros((256, 128), np.float32)
    for group, cell in enumerate((7, 4, 3, 0)):
        for source in range(2):
            for inner in range(16):
                pick[source * 128 + cell * 16 + inner, group * 32 + source * 16 + inner] = 1
    return pick


def pad_planes(slots, fetch, remote, hot, pick, table, padded):
    total = slots + REACH
    lane = lax.broadcasted_iota(jnp.int32, (slots, LANES), 1)
    for plane in range(4):
        edge = mm(jnp.concatenate([get(plane, slice(None)) for get in fetch], axis=1), pick[...]).astype(BF16)
        for j in range(8):
            rows = slice(j * slots, (j + 1) * slots)
            parts = [get(plane, rows) for get in fetch]
            table[plane, j, 0:slots, 0:128] = jnp.concatenate([part[:, 0:64] for part in parts], axis=1)
            table[plane, j, 0:slots, 128:256] = edge[rows]
            table[plane, j, 0:slots, 256:384] = jnp.concatenate([part[:, 64:128] for part in parts], axis=1)
    for plane in (0, 3):
        for j in range(8):
            parts = [ref[j] for ref in remote]
            table[plane, j, slots:total, 0:128] = jnp.concatenate([part[:, 0:64] for part in parts], axis=1)
            table[plane, j, slots:total, 128:256] = mm(jnp.concatenate(parts, axis=1), pick[...]).astype(BF16)
            table[plane, j, slots:total, 256:384] = jnp.concatenate([part[:, 64:128] for part in parts], axis=1)

    for plane in range(4):
        base = (0, 9, 9, 18)[plane]
        used = total if plane in (0, 3) else slots
        for jj in range(10):
            dy, j = ((-1, 7) if jj == 0 else (1, 0) if jj == 9 else (0, jj - 1))
            at = base + (dy + 1) * 3
            source = table[plane, j, 0:used, :]
            if plane in (1, 2) and dy == 0:
                own = source
            else:
                own = mm(hot[at + 1, :, 0:used], source).astype(BF16)
            below = mm(hot[at, :, 0:used], source[:, 128:256]).astype(BF16)
            above = mm(hot[at + 2, :, 0:used], source[:, 128:256]).astype(BF16)
            padded[plane, jj, :, 0:128] = own[:, 0:128]
            padded[plane, jj, :, 128:256] = jnp.where(lane < 32, below, jnp.where(lane < 96, own[:, 128:256], above))
            padded[plane, jj, :, 256:384] = own[:, 256:384]


def products(padded, weights, half, a_out, start):
    slots = padded.shape[2]
    for ab in range(9):
        left = padded[a_out + ab // 3, ab % 3 : ab % 3 + 8, :, half * 128 : half * 128 + 256]
        term = mm(left.reshape(8 * slots, 256), weights[half, ab])
        start = term if start is None else start + term
    return start


def even_kernel(slots, own, two, r0, r2, hot, pick, weights, sums, table, padded):
    fetch = [lambda plane, rows, ref=ref: ref[plane, rows, :] for ref in (own, two)]
    pad_planes(slots, fetch, (r0, r2), hot, pick, table, padded)
    for half in range(2):
        for a_out in range(2):
            sums[half, a_out] = products(padded, weights, half, a_out, None)


def odd_kernel(slots, chan, active, one, direct, passed, r1, r3, hot, pick, weights, down, sums, *rest):
    table, padded, stacked, answer = rest[4:]
    is_odd = (chan[0] & 1) == 1

    def three(plane, rows):
        first, second = direct[plane % 2, rows, :], passed[plane % 2, rows, :]
        return jnp.where(is_odd, second, first) if plane < 2 else jnp.where(is_odd, first, second)

    fetch = (lambda plane, rows: one[plane, rows, :], three)
    pad_planes(slots, fetch, (r1, r3), hot, pick, table, padded)
    alive = lax.broadcasted_iota(jnp.int32, (slots, 256), 0) < active[0]
    for half in range(2):
        for a_out in range(2):
            total_sum = products(padded, weights, half, a_out, sums[half, a_out])
            for j in range(8):
                block = jnp.where(alive, jnp.maximum(total_sum[j * slots : (j + 1) * slots], 0.0), 0.0).astype(BF16)
                for kk in range(2):
                    begin = ((j // 2) * 4 + half * 2 + kk) * slots
                    place = (a_out * 2 + j % 2) * 128
                    stacked[begin : begin + slots, place : place + 128] = block[:, kk * 128 : kk * 128 + 128]

    result = lax.dot_general(down[...], stacked[...], NT, preferred_element_type=F32)
    answer[...] = jnp.maximum(result, 0.0).astype(BF16)
    width = rest[0].shape[0]
    for flip in range(4):
        rest[flip][...] = answer[pl.ds(pl.multiple_of((chan[0] ^ flip) * width, width), width), :]


def even_sums(own, two, remote, hot, weights):
    slots = own.shape[1] // 8
    return pl.pallas_call(
        functools.partial(even_kernel, slots),
        out_shape=jax.ShapeDtypeStruct((2, 2, 8 * slots, 256), F32),
        in_specs=[VMEM] * 7,
        out_specs=VMEM,
        scratch_shapes=[
            pltpu.VMEM((4, 8, slots + REACH, 384), BF16),
            pltpu.VMEM((4, 10, slots, 384), BF16),
        ],
        compiler_params=params(),
        cost_estimate=pl.CostEstimate(flops=4_000_000_000, bytes_accessed=5_000_000, transcendentals=0),
        name="even_sums",
    )(own, two, *remote, hot, jnp.asarray(halo_matrix(), BF16), weights)


def convolve(chan, active, one, direct, passed, remote, hot, weights, down, sums):
    devices = 4
    slots = one.shape[1] // 8
    outputs = down.shape[0]
    return pl.pallas_call(
        functools.partial(odd_kernel, slots),
        out_shape=[jax.ShapeDtypeStruct((outputs // devices, 16 * slots), BF16)] * devices,
        in_specs=[SMEM] * 2 + [VMEM] * 10,
        out_specs=[VMEM] * devices,
        scratch_shapes=[
            pltpu.VMEM((4, 8, slots + REACH, 384), BF16),
            pltpu.VMEM((4, 10, slots, 384), BF16),
            pltpu.VMEM((16 * slots, 512), BF16),
            pltpu.VMEM((outputs, 16 * slots), BF16),
        ],
        compiler_params=params(),
        cost_estimate=pl.CostEstimate(flops=4_000_000_000, bytes_accessed=5_000_000, transcendentals=0),
        name="convolve",
    )(chan, active, one, direct, passed, *remote, hot, jnp.asarray(halo_matrix(), BF16), weights, down, sums)


def final_kernel(slots, chan, own, one, two, three, out, turned):
    outputs = own.shape[0]
    for flip, ref in enumerate((own, one, two, three)):
        plane = chan[0] ^ flip
        for cell in range(16):
            turned[pl.ds(plane * 16 + cell, outputs, stride=64), :] = ref[
                :, cell * slots : (cell + 1) * slots
            ].astype(F32)
    for tile in range(out.shape[1] // LANES):
        out[:, tile * LANES : (tile + 1) * LANES] = turned[tile * LANES : (tile + 1) * LANES, :].T.astype(BF16)


def finish(chan, coarse, others, slots):
    outputs = coarse.shape[0]
    return pl.pallas_call(
        functools.partial(final_kernel, slots),
        out_shape=jax.ShapeDtypeStruct((slots, outputs * 64), BF16),
        in_specs=[SMEM] + [VMEM] * 4,
        out_specs=VMEM,
        scratch_shapes=[pltpu.VMEM((outputs * 64, slots), F32)],
        compiler_params=params(),
        name="finish",
    )(chan, coarse, *others)


def links(adjacency, region, regions, chan, devices):
    slots = adjacency.shape[0]
    named = adjacency.T
    linked = named < slots * regions
    owner = jnp.where(linked, named // slots, regions + 7)
    slot = named % slots
    every = jnp.arange(slots, dtype=jnp.int32)
    steps = np.array([offset[0] for offset in OFFSETS])
    send_pos = []
    place = {}
    for step in (1, -1):
        rows = np.nonzero(steps == step)[0]
        owns = owner[rows[0] : rows[-1] + 1] == region + step
        sends = jnp.any(owns, axis=0)
        rank = jnp.sum((sends[None, :] & (every[None, :] < every[:, None])).astype(jnp.int32), axis=1)
        send_pos.append(jnp.where(sends, rank, -1))
        there = slot[rows[0] : rows[-1] + 1]
        member = jnp.any(owns[:, :, None] & (there[:, :, None] == every), axis=(0, 1))
        below = jnp.sum(
            (member[None, None, :] & (every < there[:, :, None])).astype(jnp.int32), axis=2
        )
        place[step] = jnp.where(owns, slots + below, -1)
    own = jnp.where(owner == region, slot, -1)
    same = jnp.concatenate([own[9:13], every[None, :], own[13:17]], axis=0)
    left = jnp.where(owner[0:9] == region, slot[0:9], place[-1])
    right = jnp.where(owner[17:26] == region, slot[17:26], place[1])
    first = jnp.where(chan == 0, left, same)
    last = jnp.where(chan == devices - 1, right, same)
    pos = jnp.concatenate([first, same, last], axis=0)
    hot = (pos[:, :, None] == jnp.arange(slots + REACH, dtype=jnp.int32)).astype(BF16)
    return jnp.stack(send_pos), hot


def send_faces(faces, regions, devices):
    got = []
    for flip in range(devices):
        other = (devices - 1) ^ flip
        pairs = [(r * devices + flip, (r + 1) * devices) for r in range(regions - 1)]
        pairs += [(r * devices + other, r * devices - 1) for r in range(1, regions)]
        got.append(lax.ppermute(faces[flip], ("region", "chan"), pairs))
    return got


def swap(value, flip, devices):
    return lax.ppermute(value, "chan", [(source, source ^ flip) for source in range(devices)])


def body(point_feats, destination, voxel_slot, adjacency, active_count, conv_weight, down_weight):
    regions = lax.axis_size("region")
    region = lax.axis_index("region")
    devices = lax.axis_size("chan")
    chan = lax.axis_index("chan")
    me = chan.reshape(1)
    slots = adjacency.shape[0]
    points = point_feats.shape[1]
    cells = slots * 512

    slot = voxel_slot // 512
    inside = voxel_slot % 512
    code = ((inside // 8) * slots + slot) * 8 + inside % 8
    keys, order = lax.sort(
        (destination * cells + code, jnp.arange(points, dtype=jnp.int32)), num_keys=1, is_stable=False
    )
    square = (points // LANES, LANES)
    taps = conv_weight.transpose(2, 3, 4, 0, 1).reshape(27, conv_weight.shape[0], -1)
    down = down_weight.transpose(1, 2, 3, 4, 0).reshape(-1, down_weight.shape[0])
    chunks, middle = exchange(
        point_feats, order.reshape(square), keys.reshape(square), region, regions, cells
    )
    mine = pack(taps, down, middle)
    late = mine[16, 0, 128] != 0
    theirs = [swap(mine, flip, devices) for flip in (1, 2, 3)]
    even, odd, down = prepare(me, mine, theirs, down_weight.shape[0])
    adjacency = jnp.where(late, 0, adjacency)

    send_pos, hot = links(adjacency, region, regions, chan, devices)
    far = far_voxels(me, chunks, regions, slots, (down, hot, send_pos))
    from_two = swap(far, 2, devices)
    near_three, near_one, near, *faces = near_voxels(me, chunks, regions, far, send_pos, slots)
    from_three = swap(near_three, 3, devices)
    from_one = swap(near_one, 1, devices)
    passed = swap(shared_planes(me, from_two), 1, devices)
    remote = send_faces(faces, regions, devices)
    sums = even_sums(near, from_two, remote[0::2], hot, even)
    coarse = convolve(me, active_count, from_one, from_three, passed, remote[1::2], hot, odd, down, sums)
    back = [swap(coarse[flip], flip, devices) for flip in (1, 2, 3)]
    return finish(me, coarse[0], back, slots)


def solution(mesh):
    return jax.shard_map(
        body,
        mesh=mesh,
        in_specs=(
            P("chan", "region"),
            P("region"),
            P("region"),
            P("region", None),
            P("region"),
            P("chan", None, None, None, None),
            P(None, "chan", None, None, None),
        ),
        out_specs=P("region", "chan"),
        check_vma=False,
    )
```

profile of v0, /device:TPU:0, one launch (start us, length us, event | category | flops | bytes accessed | tf_op | source)
XLA Modules:
  0.0 81.2 jit_solution(8973172205375513027)
XLA Ops:
  0.0 1.0 %fusion.11 = s32[16384]{0:T(1024)S(1)} fusion(s32[16384]{0:T(1024)} %param.10, s32[16384]{0:T(1024)} %param.11), kind=kLoop, calls=%fused_computation.28 | loop fusion | flops 720896 | bytes 196608 | tf_op jit(solution)/shard_map/add | solution.py:658
  1.0 6.4 %sort.15 = (s32[16384]{0:T(1024)S(1)}, s32[16384]{0:T(1024)S(1)}) sort(s32[16384]{0:T(1024)S(1)} %fusion.11, s32[16384]{0:T(1024)S(1)} %iota.21), dimensions={0}, to_apply=%region_0.1 | sort | flops 229376 | bytes 262144 | tf_op jit(solution)/shard_map/sort | solution.py:657
  7.5 0.0 copy-start.2
  7.5 1.0 %copy-done.2 = bf16[16,16384]{1,0:T(8,128)(2,1)S(1)} copy-done((bf16[16,16384]{1,0:T(8,128)(2,1)S(1)}, bf16[16,16384]{1,0:T(8,128)(2,1)}, u32[]{:S(2)}) %copy-start.2) | copy-done | bytes 524312
  8.5 2.4 %permute_piece.3 = (bf16[18,16,128]{2,1,0:T(8,128)(2,1)S(1)}, bf16[18,16,128]{2,1,0:T(8,128)(2,1)S(1)}) custom-call(s32[1]{0:T(128)} %bitcast.1.region, bf16[16,16384]{1,0:T(8,128)(2,1)S(1)} %copy-done.2, s32[128,128]{1,0:T(8,128)S(1)} %bitcast.51, s32[128,128]{1,0:T(8,128)S(1)} %bitcast.48), custom_call_target="tpu_custom_call" | custom-call | flops 2000000000 | bytes 1000000 | tf_op jit(solution)/shard_map/permute_piece/pallas_call | solution.py:132
  11.0 5.1 %collective-permute-start = (bf16[18,16,128]{2,1,0:T(8,128)(2,1)S(1)}, bf16[18,16,128]{2,1,0:T(8,128)(2,1)S(1)}, u32[]{:S(2)}, u32[]{:S(2)}) collective-permute-start(bf16[18,16,128]{2,1,0:T(8,128)(2,1)S(1)} %get-tuple-element.31), channel_id=1, source_target_pairs={{0,24},{4,28},{8,16},{12,20},{16,8},{20,12},{24,0},{28,4},{1,25},{... | collective-permute-start | bytes 221192 | tf_op jit(solution)/shard_map/ppermute | solution.py:152
  16.1 1.2 %collective-permute-start.1 = (bf16[18,16,128]{2,1,0:T(8,128)(2,1)S(1)}, bf16[18,16,128]{2,1,0:T(8,128)(2,1)S(1)}, u32[]{:S(2)}, u32[]{:S(2)}) collective-permute-start(bf16[18,16,128]{2,1,0:T(8,128)(2,1)S(1)} %get-tuple-element.32), channel_id=1, source_target_pairs={{0,28},{4,24},{8,20},{12,16},{16,12},{20,8},{24,4},{28,0},{1,29},{... | collective-permute-start | bytes 221192 | tf_op jit(solution)/shard_map/ppermute | solution.py:152
  17.2 2.4 %permute_piece.4 = (bf16[18,16,128]{2,1,0:T(8,128)(2,1)S(1)}, bf16[18,16,128]{2,1,0:T(8,128)(2,1)S(1)}) custom-call(s32[1]{0:T(128)} %bitcast.1.region, bf16[16,16384]{1,0:T(8,128)(2,1)S(1)} %copy-done.2, s32[128,128]{1,0:T(8,128)S(1)} %bitcast.52, s32[128,128]{1,0:T(8,128)S(1)} %bitcast.49), custom_call_target="tpu_custom_call" | custom-call | flops 2000000000 | bytes 1000000 | tf_op jit(solution)/shard_map/permute_piece/pallas_call | solution.py:132
  19.7 0.8 %collective-permute-start.2 = (bf16[18,16,128]{2,1,0:T(8,128)(2,1)S(1)}, bf16[18,16,128]{2,1,0:T(8,128)(2,1)S(1)}, u32[]{:S(2)}, u32[]{:S(2)}) collective-permute-start(bf16[18,16,128]{2,1,0:T(8,128)(2,1)S(1)} %get-tuple-element.33.rest_2_), channel_id=1, source_target_pairs={{0,16},{4,20},{8,24},{12,28},{16,0},{20,4},{24,8},{28,12},{1,17},{... | collective-permute-start | bytes 221192 | tf_op jit(solution)/shard_map/ppermute | solution.py:152
  20.5 2.0 %collective-permute-start.3 = (bf16[18,16,128]{2,1,0:T(8,128)(2,1)S(1)}, bf16[18,16,128]{2,1,0:T(8,128)(2,1)S(1)}, u32[]{:S(2)}, u32[]{:S(2)}) collective-permute-start(bf16[18,16,128]{2,1,0:T(8,128)(2,1)S(1)} %get-tuple-element.34), channel_id=1, source_target_pairs={{0,20},{4,16},{8,28},{12,24},{16,4},{20,0},{24,12},{28,8},{1,21},{... | collective-permute-start | bytes 221192 | tf_op jit(solution)/shard_map/ppermute | solution.py:152
  22.5 0.0 collective-permute-done.rest_0_
  22.5 0.7 collective-permute-done.1.rest_1_
  23.2 4.6 %permute_piece.5 = (bf16[18,16,128]{2,1,0:T(8,128)(2,1)S(1)}, bf16[18,16,128]{2,1,0:T(8,128)(2,1)S(1)}, bf16[18,16,128]{2,1,0:T(8,128)(2,1)S(1)}, bf16[18,16,128]{2,1,0:T(8,128)(2,1)S(1)}) custom-call(s32[1]{0:T(128)} %bitcast.1.region, bf16[16,16384]{1,0:T(8,128)(2,1)S(1)} %copy-done.3, s32[128,128]{1,0:T(8,128)S(1)} %bitcast.53, s32[128,128]{1,0:T(8,128)S(1)} %bitcast.50, ...), custom_call_target="tpu_custom_call" | custom-call | flops 2000000000 | bytes 1000000 | tf_op jit(solution)/shard_map/permute_piece/pallas_call | solution.py:132
  27.8 0.2 copy-done
  28.0 0.1 pack.1.own
  28.1 0.5 slice.32
  28.6 0.0 collective-permute-start.7
  28.7 1.5 %collective-permute-start.8 = (bf16[17,16,192]{2,1,0:T(8,128)(2,1)S(1)}, bf16[17,16,192]{2,1,0:T(8,128)(2,1)S(1)}, u32[]{:S(2)}, u32[]{:S(2)}) collective-permute-start(bf16[17,16,192]{2,1,0:T(8,128)(2,1)S(1)} %pack.1.own), channel_id=1, source_target_pairs={{0,2},{1,3},{2,0},{3,1},{4,6},{5,7},{6,4},{7,5},{8,10},{9,11},{10,... | collective-permute-start | bytes 313352 | tf_op jit(solution)/shard_map/ppermute | solution.py:641
  30.2 0.3 collective-permute-start.9
  31.2 0.1 convert_reduce_fusion.2
  31.3 0.5 fusion.2
  31.8 0.4 convert_reduce_fusion.1
  32.2 0.4 convert_reduce_fusion
  32.6 0.2 concatenate.8
  32.8 0.3 fusion.rest_9_.hot
  33.1 0.0 collective-permute-done.7.one
  33.2 0.8 %collective-permute-start.4 = (bf16[18,16,128]{2,1,0:T(8,128)(2,1)S(1)}, bf16[18,16,128]{2,1,0:T(8,128)(2,1)S(1)}, u32[]{:S(2)}, u32[]{:S(2)}) collective-permute-start(bf16[18,16,128]{2,1,0:T(8,128)(2,1)S(1)} %get-tuple-element.35._), channel_id=1, source_target_pairs={{0,8},{4,12},{8,0},{12,4},{16,24},{20,28},{24,16},{28,20},{1,9},{5... | collective-permute-start | bytes 221192 | tf_op jit(solution)/shard_map/ppermute | solution.py:152
  34.0 1.2 %collective-permute-done.8.two = bf16[17,16,192]{2,1,0:T(8,128)(2,1)S(1)} collective-permute-done((bf16[17,16,192]{2,1,0:T(8,128)(2,1)S(1)}, bf16[17,16,192]{2,1,0:T(8,128)(2,1)S(1)}, u32[]{:S(2)}, u32[]{:S(2)}) %collective-permute-start.8) | collective-permute-done | bytes 104480 | tf_op jit(solution)/shard_map/ppermute | solution.py:641
  35.1 2.2 %collective-permute-start.5 = (bf16[18,16,128]{2,1,0:T(8,128)(2,1)S(1)}, bf16[18,16,128]{2,1,0:T(8,128)(2,1)S(1)}, u32[]{:S(2)}, u32[]{:S(2)}) collective-permute-start(bf16[18,16,128]{2,1,0:T(8,128)(2,1)S(1)} %get-tuple-element.36), channel_id=1, source_target_pairs={{0,12},{4,8},{8,4},{12,0},{16,28},{20,24},{24,20},{28,16},{1,13},{... | collective-permute-start | bytes 221192 | tf_op jit(solution)/shard_map/ppermute | solution.py:152
  37.3 0.0 collective-permute-done.9.three
  37.3 1.4 %collective-permute-start.6 = (bf16[18,16,128]{2,1,0:T(8,128)(2,1)S(1)}, bf16[18,16,128]{2,1,0:T(8,128)(2,1)S(1)}, u32[]{:S(2)}, u32[]{:S(2)}) collective-permute-start(bf16[18,16,128]{2,1,0:T(8,128)(2,1)S(1)} %get-tuple-element.37), channel_id=1, source_target_pairs={{0,4},{4,0},{8,12},{12,8},{16,20},{20,16},{24,28},{28,24},{1,5},{5... | collective-permute-start | bytes 221192 | tf_op jit(solution)/shard_map/ppermute | solution.py:152
  38.8 1.5 %prepare.1 = (bf16[2,9,256,256]{3,2,1,0:T(8,128)(2,1)S(1)}, bf16[2,9,256,256]{3,2,1,0:T(8,128)(2,1)S(1)}, bf16[128,512]{1,0:T(8,128)(2,1)S(1)}) custom-call(s32[1]{0:T(128)} %bitcast.chan, bf16[17,16,192]{2,1,0:T(8,128)(2,1)S(1)} %pack.1.own, bf16[17,16,192]{2,1,0:T(8,128)(2,1)S(1)} %collective-permute-done.7.one, ...), custom_call_target="tpu_custom_call" | custom-call | flops 2000000000 | bytes 3000000 | tf_op jit(solution)/shard_map/prepare/pallas_call | solution.py:429
  40.3 0.0 collective-permute-done.2.rest_2_
  40.3 0.0 collective-permute-done.3.rest_3_
  40.3 0.0 collective-permute-done.4.rest_4_
  40.3 0.0 collective-permute-done.5.rest_5_
  40.4 1.6 %collective-permute-done.6.rest_6_ = bf16[18,16,128]{2,1,0:T(8,128)(2,1)S(1)} collective-permute-done((bf16[18,16,128]{2,1,0:T(8,128)(2,1)S(1)}, bf16[18,16,128]{2,1,0:T(8,128)(2,1)S(1)}, u32[]{:S(2)}, u32[]{:S(2)}) %collective-permute-start.6) | collective-permute-done | bytes 73760 | tf_op jit(solution)/shard_map/ppermute | solution.py:152
  42.0 4.9 %far_voxels.1.rest_8_ = bf16[4,512,128]{2,1,0:T(8,128)(2,1)S(1)} custom-call(s32[1]{0:T(128)} %bitcast.chan, bf16[18,16,128]{2,1,0:T(8,128)(2,1)S(1)} %collective-permute-done.rest_0_, bf16[18,16,128]{2,1,0:T(8,128)(2,1)S(1)} %collective-permute-done.1.rest_1_, bf16[18,16,128]{2,1,0:T(8,128)(2,1)S(1)} %collective-permute-done.2.rest_2_, ...), custom_call_target="tpu_custom_call" | custom-call | flops 4000000000 | bytes 1200000 | tf_op jit(solution)/shard_map/far_voxels/pallas_call | solution.py:327
  46.8 0.0 copy-start.4
  46.8 1.6 %collective-permute-start.12 = (bf16[4,512,128]{2,1,0:T(8,128)(2,1)S(1)}, bf16[4,512,128]{2,1,0:T(8,128)(2,1)S(1)}, u32[]{:S(2)}, u32[]{:S(2)}) collective-permute-start(bf16[4,512,128]{2,1,0:T(8,128)(2,1)S(1)} %far_voxels.1.rest_8_), channel_id=1, source_target_pairs={{0,2},{1,3},{2,0},{3,1},{4,6},{5,7},{6,4},{7,5},{8,10},{9,11},{10,... | collective-permute-start | bytes 1572872 | tf_op jit(solution)/shard_map/ppermute | solution.py:641
  48.4 5.4 %near_voxels.1 = (bf16[2,512,128]{2,1,0:T(8,128)(2,1)S(1)}, bf16[4,512,128]{2,1,0:T(8,128)(2,1)S(1)}, bf16[4,512,128]{2,1,0:T(8,128)(2,1)S(1)}, bf16[8,16,128]{2...) custom-call(s32[1]{0:T(128)} %bitcast.chan, ...), custom_call_target="tpu_custom_call" | custom-call | flops 4000000000 | bytes 3000000 | tf_op jit(solution)/shard_map/near_voxels/pallas_call | solution.py:340
  53.8 0.1 collective-permute-start.10
  53.9 3.4 %collective-permute-start.16 = (bf16[8,16,128]{2,1,0:T(8,128)(2,1)S(1)}, bf16[8,16,128]{2,1,0:T(8,128)(2,1)S(1)}, u32[]{:S(2)}, u32[]{:S(2)}) collective-permute-start(bf16[8,16,128]{2,1,0:T(8,128)(2,1)S(1)} %get-tuple-element.46), channel_id=1, source_target_pairs={{0,4},{4,8},{8,12},{12,16},{16,20},{20,24},{24,28},{7,3},{11,7},{1... | collective-permute-start | bytes 98312 | tf_op jit(solution)/shard_map/ppermute | solution.py:636
  57.3 0.7 collective-permute-start.17
  58.6 0.1 collective-permute-start.11
  58.7 1.7 %collective-permute-done.12.planes.two = bf16[4,512,128]{2,1,0:T(8,128)(2,1)S(1)} collective-permute-done((bf16[4,512,128]{2,1,0:T(8,128)(2,1)S(1)}, bf16[4,512,128]{2,1,0:T(8,128)(2,1)S(1)}, u32[]{:S(2)}, u32[]{:S(2)}) %collective-permute-start.12) | collective-permute-done | bytes 524320 | tf_op jit(solution)/shard_map/ppermute | solution.py:641
  60.4 0.7 collective-permute-start.14
  61.1 0.0 collective-permute-done.16.r0
  61.1 0.7 collective-permute-start.15
  61.8 0.0 collective-permute-done.17.r2
  61.8 3.0 %collective-permute-start.13 = (bf16[2,512,128]{2,1,0:T(8,128)(2,1)S(1)}, bf16[2,512,128]{2,1,0:T(8,128)(2,1)S(1)}, u32[]{:S(2)}, u32[]{:S(2)}) collective-permute-start(bf16[2,512,128]{2,1,0:T(8,128)(2,1)S(1)} %shared_planes.1), channel_id=1, source_target_pairs={{0,1},{1,0},{2,3},{3,2},{4,5},{5,4},{6,7},{7,6},{8,9},{9,8},{10,11... | collective-permute-start | bytes 786440 | tf_op jit(solution)/shard_map/ppermute | solution.py:641
  64.8 3.9 %even_sums.1.sums = f32[2,2,512,256]{3,2,1,0:T(8,128)S(1)} custom-call(bf16[4,512,128]{2,1,0:T(8,128)(2,1)S(1)} %get-tuple-element.45.own, bf16[4,512,128]{2,1,0:T(8,128)(2,1)S(1)} %collective-permute-done.12.planes.two, bf16[8,16,128]{2,1,0:T(8,128)(2,1)S(1)} %collective-permute-done.16.r0, bf16[8,16,128]{2,1,0:T(8,128)(2,1)S(1)} %collective-permute-done.17.r2, ...), custom_call_target="tpu_custom_call" | custom-call | flops 4000000000 | bytes 5000000 | tf_op jit(solution)/shard_map/even_sums/pallas_call | solution.py:536
  68.7 0.0 collective-permute-done.14.r1
  68.7 0.0 collective-permute-done.15.r3
  68.7 0.0 collective-permute-done.11.direct
  68.7 0.0 collective-permute-done.10.one
  68.7 0.0 collective-permute-done.13.passed
  68.7 4.3 %convolve.1 = (bf16[32,1024]{1,0:T(8,128)(2,1)S(1)}, bf16[32,1024]{1,0:T(8,128)(2,1)S(1)}, bf16[32,1024]{1,0:T(8,128)(2,1)S(1)}, bf16[32,1024]{1,0:T(8,128)(2,1)S(1)}) custom-call(s32[1]{0:T(128)} %bitcast.chan, s32[1]{0:T(128)S(6)} %copy.10.active, bf16[4,512,128]{2,1,0:T(8,128)(2,1)S(1)} %collective-permute-done.10.one, ...), custom_call_target="tpu_custom_call" | custom-call | flops 4000000000 | bytes 5000000 | tf_op jit(solution)/shard_map/convolve/pallas_call | solution.py:555
  73.0 0.1 collective-permute-start.18
  73.1 2.1 %collective-permute-start.19 = (bf16[32,1024]{1,0:T(8,128)(2,1)S(1)}, bf16[32,1024]{1,0:T(8,128)(2,1)S(1)}, u32[]{:S(2)}, u32[]{:S(2)}) collective-permute-start(bf16[32,1024]{1,0:T(8,128)(2,1)S(1)} %get-tuple-element.51), channel_id=1, source_target_pairs={{0,2},{1,3},{2,0},{3,1},{4,6},{5,7},{6,4},{7,5},{8,10},{9,11},{10,... | collective-permute-start | bytes 196616 | tf_op jit(solution)/shard_map/ppermute | solution.py:641
  75.2 0.1 collective-permute-start.20
  75.3 2.6 %collective-permute-done.19.two = bf16[32,1024]{1,0:T(8,128)(2,1)S(1)} collective-permute-done((bf16[32,1024]{1,0:T(8,128)(2,1)S(1)}, bf16[32,1024]{1,0:T(8,128)(2,1)S(1)}, u32[]{:S(2)}, u32[]{:S(2)}) %collective-permute-start.19) | collective-permute-done | bytes 65568 | tf_op jit(solution)/shard_map/ppermute | solution.py:641
  77.9 1.4 %collective-permute-done.20.three = bf16[32,1024]{1,0:T(8,128)(2,1)S(1)} collective-permute-done((bf16[32,1024]{1,0:T(8,128)(2,1)S(1)}, bf16[32,1024]{1,0:T(8,128)(2,1)S(1)}, u32[]{:S(2)}, u32[]{:S(2)}) %collective-permute-start.20) | collective-permute-done | bytes 65568 | tf_op jit(solution)/shard_map/ppermute | solution.py:641
  79.3 1.9 %finish.1 = bf16[64,2048]{1,0:T(8,128)(2,1)} custom-call(s32[1]{0:T(128)} %bitcast.chan, bf16[32,1024]{1,0:T(8,128)(2,1)S(1)} %get-tuple-element.49.own, bf16[32,1024]{1,0:T(8,128)(2,1)S(1)} %collective-permute-done.18.one, bf16[32,1024]{1,0:T(8,128)(2,1)S(1)} %collective-permute-done.19.two, bf16[32,1024]{1,0:T(8,128)(2,1)S(1)} %collective-permute-done.20.three), custom_call_target="tpu_custom_call" | custom-call | tf_op jit(solution)/shard_map/finish/pallas_call | solution.py:586
  (21 shorter events, 0.2 us)
Async XLA Ops:
  7.5 1.0 %copy-start.2 = (bf16[16,16384]{1,0:T(8,128)(2,1)S(1)}, bf16[16,16384]{1,0:T(8,128)(2,1)}, u32[]{:S(2)}) copy-start(bf16[16,16384]{1,0:T(8,128)(2,1)} %feats.5) | copy-start | bytes 1572868
  11.0 11.5 %collective-permute-start = (bf16[18,16,128]{2,1,0:T(8,128)(2,1)S(1)}, bf16[18,16,128]{2,1,0:T(8,128)(2,1)S(1)}, u32[]{:S(2)}, u32[]{:S(2)}) collective-permute-start(bf16[18,16,128]{2,1,0:T(8,128)(2,1)S(1)} %get-tuple-element.31), channel_id=1, source_target_pairs={{0,24},{4,28},{8,16},{12,20},{16,8},{20,12},{24,0},{28,4},{1,25},{... | collective-permute-start | bytes 221192 | tf_op jit(solution)/shard_map/ppermute | solution.py:152
  16.1 7.2 %copy-start.3 = (bf16[16,16384]{1,0:T(8,128)(2,1)S(1)}, bf16[16,16384]{1,0:T(8,128)(2,1)}, u32[]{:S(2)}) copy-start(bf16[16,16384]{1,0:T(8,128)(2,1)} %feats.5) | copy-start | bytes 1572868
  16.1 7.2 %collective-permute-start.1 = (bf16[18,16,128]{2,1,0:T(8,128)(2,1)S(1)}, bf16[18,16,128]{2,1,0:T(8,128)(2,1)S(1)}, u32[]{:S(2)}, u32[]{:S(2)}) collective-permute-start(bf16[18,16,128]{2,1,0:T(8,128)(2,1)S(1)} %get-tuple-element.32), channel_id=1, source_target_pairs={{0,28},{4,24},{8,20},{12,16},{16,12},{20,8},{24,4},{28,0},{1,29},{... | collective-permute-start | bytes 221192 | tf_op jit(solution)/shard_map/ppermute | solution.py:152
  19.7 20.6 %collective-permute-start.2 = (bf16[18,16,128]{2,1,0:T(8,128)(2,1)S(1)}, bf16[18,16,128]{2,1,0:T(8,128)(2,1)S(1)}, u32[]{:S(2)}, u32[]{:S(2)}) collective-permute-start(bf16[18,16,128]{2,1,0:T(8,128)(2,1)S(1)} %get-tuple-element.33.rest_2_), channel_id=1, source_target_pairs={{0,16},{4,20},{8,24},{12,28},{16,0},{20,4},{24,8},{28,12},{1,17},{... | collective-permute-start | bytes 221192 | tf_op jit(solution)/shard_map/ppermute | solution.py:152
  20.5 19.8 %collective-permute-start.3 = (bf16[18,16,128]{2,1,0:T(8,128)(2,1)S(1)}, bf16[18,16,128]{2,1,0:T(8,128)(2,1)S(1)}, u32[]{:S(2)}, u32[]{:S(2)}) collective-permute-start(bf16[18,16,128]{2,1,0:T(8,128)(2,1)S(1)} %get-tuple-element.34), channel_id=1, source_target_pairs={{0,20},{4,16},{8,28},{12,24},{16,4},{20,0},{24,12},{28,8},{1,21},{... | collective-permute-start | bytes 221192 | tf_op jit(solution)/shard_map/ppermute | solution.py:152
  22.5 5.5 %copy-start = (bf16[16,64,3,3,3]{1,0,4,3,2:T(8,128)(2,1)S(1)}, bf16[16,64,3,3,3]{1,0,4,3,2:T(8,128)(2,1)}, u32[]{:S(2)}) copy-start(bf16[16,64,3,3,3]{1,0,4,3,2:T(8,128)(2,1)} %param.14) | copy-start | bytes 165892
  22.5 5.5 %copy-start.1 = (bf16[128,16,2,2,2]{0,4,3,2,1:T(2,128)(2,1)S(1)}, bf16[128,16,2,2,2]{0,4,3,2,1:T(2,128)(2,1)}, u32[]{:S(2)}) copy-start(bf16[128,16,2,2,2]{0,4,3,2,1:T(2,128)(2,1)} %param.15) | copy-start | bytes 98308
  22.5 8.6 %copy-start.5 = (s32[64,26]{0,1:T(8,128)S(1)}, s32[64,26]{0,1:T(8,128)}, u32[]{:S(2)}) copy-start(s32[64,26]{0,1:T(8,128)} %param.12) | copy-start | bytes 19972
  28.6 4.5 %collective-permute-start.7 = (bf16[17,16,192]{2,1,0:T(8,128)(2,1)S(1)}, bf16[17,16,192]{2,1,0:T(8,128)(2,1)S(1)}, u32[]{:S(2)}, u32[]{:S(2)}) collective-permute-start(bf16[17,16,192]{2,1,0:T(8,128)(2,1)S(1)} %pack.1.own), channel_id=1, source_target_pairs={{0,1},{1,0},{2,3},{3,2},{4,5},{5,4},{6,7},{7,6},{8,9},{9,8},{10,11... | collective-permute-start | bytes 313352 | tf_op jit(solution)/shard_map/ppermute | solution.py:641
  28.7 6.5 %collective-permute-start.8 = (bf16[17,16,192]{2,1,0:T(8,128)(2,1)S(1)}, bf16[17,16,192]{2,1,0:T(8,128)(2,1)S(1)}, u32[]{:S(2)}, u32[]{:S(2)}) collective-permute-start(bf16[17,16,192]{2,1,0:T(8,128)(2,1)S(1)} %pack.1.own), channel_id=1, source_target_pairs={{0,2},{1,3},{2,0},{3,1},{4,6},{5,7},{6,4},{7,5},{8,10},{9,11},{10,... | collective-permute-start | bytes 313352 | tf_op jit(solution)/shard_map/ppermute | solution.py:641
  30.2 7.2 %collective-permute-start.9 = (bf16[17,16,192]{2,1,0:T(8,128)(2,1)S(1)}, bf16[17,16,192]{2,1,0:T(8,128)(2,1)S(1)}, u32[]{:S(2)}, u32[]{:S(2)}) collective-permute-start(bf16[17,16,192]{2,1,0:T(8,128)(2,1)S(1)} %pack.1.own), channel_id=1, source_target_pairs={{0,3},{1,2},{2,1},{3,0},{4,7},{5,6},{6,5},{7,4},{8,11},{9,10},{10,... | collective-permute-start | bytes 313352 | tf_op jit(solution)/shard_map/ppermute | solution.py:641
  33.2 7.2 %collective-permute-start.4 = (bf16[18,16,128]{2,1,0:T(8,128)(2,1)S(1)}, bf16[18,16,128]{2,1,0:T(8,128)(2,1)S(1)}, u32[]{:S(2)}, u32[]{:S(2)}) collective-permute-start(bf16[18,16,128]{2,1,0:T(8,128)(2,1)S(1)} %get-tuple-element.35._), channel_id=1, source_target_pairs={{0,8},{4,12},{8,0},{12,4},{16,24},{20,28},{24,16},{28,20},{1,9},{5... | collective-permute-start | bytes 221192 | tf_op jit(solution)/shard_map/ppermute | solution.py:152
  35.1 5.3 %collective-permute-start.5 = (bf16[18,16,128]{2,1,0:T(8,128)(2,1)S(1)}, bf16[18,16,128]{2,1,0:T(8,128)(2,1)S(1)}, u32[]{:S(2)}, u32[]{:S(2)}) collective-permute-start(bf16[18,16,128]{2,1,0:T(8,128)(2,1)S(1)} %get-tuple-element.36), channel_id=1, source_target_pairs={{0,12},{4,8},{8,4},{12,0},{16,28},{20,24},{24,20},{28,16},{1,13},{... | collective-permute-start | bytes 221192 | tf_op jit(solution)/shard_map/ppermute | solution.py:152
  37.3 4.6 %collective-permute-start.6 = (bf16[18,16,128]{2,1,0:T(8,128)(2,1)S(1)}, bf16[18,16,128]{2,1,0:T(8,128)(2,1)S(1)}, u32[]{:S(2)}, u32[]{:S(2)}) collective-permute-start(bf16[18,16,128]{2,1,0:T(8,128)(2,1)S(1)} %get-tuple-element.37), channel_id=1, source_target_pairs={{0,4},{4,0},{8,12},{12,8},{16,20},{20,16},{24,28},{28,24},{1,5},{5... | collective-permute-start | bytes 221192 | tf_op jit(solution)/shard_map/ppermute | solution.py:152
  46.8 17.9 %copy-start.4 = (bf16[256,128]{1,0:T(8,128)(2,1)S(1)}, bf16[256,128]{1,0:T(8,128)(2,1)}, u32[]{:S(2)}) copy-start(bf16[256,128]{1,0:T(8,128)(2,1)} %constant.101.clone.pick) | copy-start | bytes 196612
  46.8 13.5 %collective-permute-start.12 = (bf16[4,512,128]{2,1,0:T(8,128)(2,1)S(1)}, bf16[4,512,128]{2,1,0:T(8,128)(2,1)S(1)}, u32[]{:S(2)}, u32[]{:S(2)}) collective-permute-start(bf16[4,512,128]{2,1,0:T(8,128)(2,1)S(1)} %far_voxels.1.rest_8_), channel_id=1, source_target_pairs={{0,2},{1,3},{2,0},{3,1},{4,6},{5,7},{6,4},{7,5},{8,10},{9,11},{10,... | collective-permute-start | bytes 1572872 | tf_op jit(solution)/shard_map/ppermute | solution.py:641
  53.8 14.9 %collective-permute-start.10 = (bf16[4,512,128]{2,1,0:T(8,128)(2,1)S(1)}, bf16[4,512,128]{2,1,0:T(8,128)(2,1)S(1)}, u32[]{:S(2)}, u32[]{:S(2)}) collective-permute-start(bf16[4,512,128]{2,1,0:T(8,128)(2,1)S(1)} %get-tuple-element.40), channel_id=1, source_target_pairs={{0,1},{1,0},{2,3},{3,2},{4,5},{5,4},{6,7},{7,6},{8,9},{9,8},{10,11... | collective-permute-start | bytes 1572872 | tf_op jit(solution)/shard_map/ppermute | solution.py:641
  53.9 7.2 %collective-permute-start.16 = (bf16[8,16,128]{2,1,0:T(8,128)(2,1)S(1)}, bf16[8,16,128]{2,1,0:T(8,128)(2,1)S(1)}, u32[]{:S(2)}, u32[]{:S(2)}) collective-permute-start(bf16[8,16,128]{2,1,0:T(8,128)(2,1)S(1)} %get-tuple-element.46), channel_id=1, source_target_pairs={{0,4},{4,8},{8,12},{12,16},{16,20},{20,24},{24,28},{7,3},{11,7},{1... | collective-permute-start | bytes 98312 | tf_op jit(solution)/shard_map/ppermute | solution.py:636
  57.3 4.5 %collective-permute-start.17 = (bf16[8,16,128]{2,1,0:T(8,128)(2,1)S(1)}, bf16[8,16,128]{2,1,0:T(8,128)(2,1)S(1)}, u32[]{:S(2)}, u32[]{:S(2)}) collective-permute-start(bf16[8,16,128]{2,1,0:T(8,128)(2,1)S(1)} %get-tuple-element.47), channel_id=1, source_target_pairs={{2,4},{6,8},{10,12},{14,16},{18,20},{22,24},{26,28},{5,3},{9,7},{1... | collective-permute-start | bytes 98312 | tf_op jit(solution)/shard_map/ppermute | solution.py:636
  58.6 10.1 %collective-permute-start.11 = (bf16[2,512,128]{2,1,0:T(8,128)(2,1)S(1)}, bf16[2,512,128]{2,1,0:T(8,128)(2,1)S(1)}, u32[]{:S(2)}, u32[]{:S(2)}) collective-permute-start(bf16[2,512,128]{2,1,0:T(8,128)(2,1)S(1)} %get-tuple-element.41), channel_id=1, source_target_pairs={{0,3},{1,2},{2,1},{3,0},{4,7},{5,6},{6,5},{7,4},{8,11},{9,10},{10,... | collective-permute-start | bytes 786440 | tf_op jit(solution)/shard_map/ppermute | solution.py:641
  60.4 8.3 %collective-permute-start.14 = (bf16[8,16,128]{2,1,0:T(8,128)(2,1)S(1)}, bf16[8,16,128]{2,1,0:T(8,128)(2,1)S(1)}, u32[]{:S(2)}, u32[]{:S(2)}) collective-permute-start(bf16[8,16,128]{2,1,0:T(8,128)(2,1)S(1)} %get-tuple-element.42), channel_id=1, source_target_pairs={{1,4},{5,8},{9,12},{13,16},{17,20},{21,24},{25,28},{6,3},{10,7},{1... | collective-permute-start | bytes 98312 | tf_op jit(solution)/shard_map/ppermute | solution.py:636
  61.1 7.6 %collective-permute-start.15 = (bf16[8,16,128]{2,1,0:T(8,128)(2,1)S(1)}, bf16[8,16,128]{2,1,0:T(8,128)(2,1)S(1)}, u32[]{:S(2)}, u32[]{:S(2)}) collective-permute-start(bf16[8,16,128]{2,1,0:T(8,128)(2,1)S(1)} %get-tuple-element.43), channel_id=1, source_target_pairs={{3,4},{7,8},{11,12},{15,16},{19,20},{23,24},{27,28},{4,3},{8,7},{1... | collective-permute-start | bytes 98312 | tf_op jit(solution)/shard_map/ppermute | solution.py:636
  61.8 6.9 %collective-permute-start.13 = (bf16[2,512,128]{2,1,0:T(8,128)(2,1)S(1)}, bf16[2,512,128]{2,1,0:T(8,128)(2,1)S(1)}, u32[]{:S(2)}, u32[]{:S(2)}) collective-permute-start(bf16[2,512,128]{2,1,0:T(8,128)(2,1)S(1)} %shared_planes.1), channel_id=1, source_target_pairs={{0,1},{1,0},{2,3},{3,2},{4,5},{5,4},{6,7},{7,6},{8,9},{9,8},{10,11... | collective-permute-start | bytes 786440 | tf_op jit(solution)/shard_map/ppermute | solution.py:641
  73.0 2.3 %collective-permute-start.18 = (bf16[32,1024]{1,0:T(8,128)(2,1)S(1)}, bf16[32,1024]{1,0:T(8,128)(2,1)S(1)}, u32[]{:S(2)}, u32[]{:S(2)}) collective-permute-start(bf16[32,1024]{1,0:T(8,128)(2,1)S(1)} %get-tuple-element.50), channel_id=1, source_target_pairs={{0,1},{1,0},{2,3},{3,2},{4,5},{5,4},{6,7},{7,6},{8,9},{9,8},{10,11... | collective-permute-start | bytes 196616 | tf_op jit(solution)/shard_map/ppermute | solution.py:641
  73.1 4.8 %collective-permute-start.19 = (bf16[32,1024]{1,0:T(8,128)(2,1)S(1)}, bf16[32,1024]{1,0:T(8,128)(2,1)S(1)}, u32[]{:S(2)}, u32[]{:S(2)}) collective-permute-start(bf16[32,1024]{1,0:T(8,128)(2,1)S(1)} %get-tuple-element.51), channel_id=1, source_target_pairs={{0,2},{1,3},{2,0},{3,1},{4,6},{5,7},{6,4},{7,5},{8,10},{9,11},{10,... | collective-permute-start | bytes 196616 | tf_op jit(solution)/shard_map/ppermute | solution.py:641
  75.2 4.0 %collective-permute-start.20 = (bf16[32,1024]{1,0:T(8,128)(2,1)S(1)}, bf16[32,1024]{1,0:T(8,128)(2,1)S(1)}, u32[]{:S(2)}, u32[]{:S(2)}) collective-permute-start(bf16[32,1024]{1,0:T(8,128)(2,1)S(1)} %get-tuple-element.52), channel_id=1, source_target_pairs={{0,3},{1,2},{2,1},{3,0},{4,7},{5,6},{6,5},{7,4},{8,11},{9,10},{10,... | collective-permute-start | bytes 196616 | tf_op jit(solution)/shard_map/ppermute | solution.py:641
where the time goes:
time: 82.1 us; the launch traced here: 81.2 us
  Pallas kernels  31.4 us (38%)
  starting transfers between devices  27.8 us (34%)
  waiting for transfers between devices  9.22 us (11%)
  other arithmetic  9.16 us (11%)
  local copies, waits for them, and re-layouts  2 us (2%)
  between operations  1.58 us (2%)
    ppermute x7, starting transfers between devices, send(): lax.ppermute(value, 'region', pair)  13.6 us
    pallas_call x3, Pallas kernels, permute_piece(): pl.pallas_call(functools.partial(piece_kernel, depth, cells, flips), out_...  9.48 us
    ppermute x10, starting transfers between devices, swap(): lax.ppermute(value, 'chan', [(source, source ^ flip) for source in range(...  8.87 us
    ppermute x10, waiting for transfers between devices, swap(): lax.ppermute(value, 'chan', [(source, source ^ flip) for source in range(...  6.84 us
    sort x1, other arithmetic, body(): lax.sort((destination * cells + code, jnp.arange(points, dtype=jnp.int32)...  6.45 us
    pallas_call x1, Pallas kernels, near_voxels(): pl.pallas_call(functools.partial(near_kernel, slots, len(chunks)), out_sh...  5.38 us
    ppermute x4, starting transfers between devices, send_faces(): got.append(lax.ppermute(faces[flip], ('region', 'chan'), pairs))  5.37 us
    pallas_call x1, Pallas kernels, far_voxels(): pl.pallas_call(functools.partial(far_kernel, len(chunks)), out_shape=jax....  4.86 us
  transfers between devices with their start and end apart: 21, of which 6 were waited for; matrix products, arithmetic and copies ran while one was open for 3% of the time, Pallas kernels for 22%

commit v1 on v0

--- a/solution.py
+++ b/solution.py
@@ -155,12 +155,12 @@
     made = []
     got = []
     for number, flips in enumerate(((6, 7), (4, 5), (2, 3, 1, 0))):
-        before = [*got[number - 2], made[-1][0]] if number >= 2 else ()
+        before = [values[0] for values in made[-1:]] + (got[number - 2] if number >= 2 else [])
         values = permute_piece(flips, at, feats, order, keys, regions, cells, before)
         made.append(values)
         sent = sum(flip != 0 for flip in flips)
         got.append(send(values[:sent], flips[:sent]) + list(values[sent:]))
-    return [chunk for some in got for chunk in some], made[2][0]
+    return [chunk for some in got for chunk in some], made[1][0]
 
 
 WINDOW = 256
@@ -594,37 +594,54 @@
     )(chan, coarse, *others)
 
 
-def links(adjacency, region, regions, chan, devices):
+def link_kernel(regions, place_of, named, _, send_pos, hot):
+    slots = named.shape[1]
+    region, chan = place_of[0], place_of[1]
+    names = named[...]
+    owner = jnp.where(names < slots * regions, names >> (slots.bit_length() - 1), regions + 7)
+    slot = names & (slots - 1)
+    row = lax.broadcasted_iota(jnp.int32, (slots, slots), 0)
+    earlier = jnp.where(row < lax.broadcasted_iota(jnp.int32, (slots, slots), 1), 1.0, 0.0).astype(BF16)
+    far = {}
+    for number, (step, begin) in enumerate(((1, 17), (-1, 0))):
+        numbers = range(begin, begin + 9)
+        owns = {n: jnp.where(owner[n : n + 1] == region + step, 1.0, 0.0) for n in numbers}
+        sends = functools.reduce(jnp.maximum, owns.values())
+        rank = mm(jnp.broadcast_to(sends, (16, slots)).astype(BF16), earlier)[0:1]
+        send_pos[number : number + 1, :] = jnp.where(sends > 0.0, rank, -1.0).astype(jnp.int32)
+        member = jnp.zeros((slots, 1), F32)
+        for n in numbers:
+            hit = jnp.where(row == slot[n : n + 1], owns[n], 0.0)
+            member = jnp.maximum(member, jnp.max(hit, axis=1, keepdims=True))
+        for n in numbers:
+            below = jnp.sum(jnp.where(row < slot[n : n + 1], member, 0.0), axis=0, keepdims=True)
+            far[n] = jnp.where(owns[n] > 0.0, slots + below, -1.0).astype(jnp.int32)
+    every = lax.broadcasted_iota(jnp.int32, (1, slots), 1)
+    own = {n: jnp.where(owner[n : n + 1] == region, slot[n : n + 1], -1) for n in range(26)}
+    same = [own[n] for n in range(9, 13)] + [every] + [own[n] for n in range(13, 17)]
+    left = [jnp.maximum(own[n], far[n]) for n in range(0, 9)]
+    right = [jnp.maximum(own[n], far[n]) for n in range(17, 26)]
+    first = [jnp.where(chan == 0, *both) for both in zip(left, same)]
+    last = [jnp.where(chan == 3, *both) for both in zip(right, same)]
+    entry = lax.broadcasted_iota(jnp.int32, (LANES, slots), 0)
+    for number, pos in enumerate(first + same + last):
+        turned = jnp.where(entry == pos, 1.0, 0.0).T.astype(BF16)
+        hot[number] = turned[:, : slots + REACH]
+
+
+def links(adjacency, region, regions, chan, before):
     slots = adjacency.shape[0]
-    named = adjacency.T
-    linked = named < slots * regions
-    owner = jnp.where(linked, named // slots, regions + 7)
-    slot = named % slots
-    every = jnp.arange(slots, dtype=jnp.int32)
-    steps = np.array([offset[0] for offset in OFFSETS])
-    send_pos = []
-    place = {}
-    for step in (1, -1):
-        rows = np.nonzero(steps == step)[0]
-        owns = owner[rows[0] : rows[-1] + 1] == region + step
-        sends = jnp.any(owns, axis=0)
-        rank = jnp.sum((sends[None, :] & (every[None, :] < every[:, None])).astype(jnp.int32), axis=1)
-        send_pos.append(jnp.where(sends, rank, -1))
-        there = slot[rows[0] : rows[-1] + 1]
-        member = jnp.any(owns[:, :, None] & (there[:, :, None] == every), axis=(0, 1))
-        below = jnp.sum(
-            (member[None, None, :] & (every < there[:, :, None])).astype(jnp.int32), axis=2
-        )
-        place[step] = jnp.where(owns, slots + below, -1)
-    own = jnp.where(owner == region, slot, -1)
-    same = jnp.concatenate([own[9:13], every[None, :], own[13:17]], axis=0)
-    left = jnp.where(owner[0:9] == region, slot[0:9], place[-1])
-    right = jnp.where(owner[17:26] == region, slot[17:26], place[1])
-    first = jnp.where(chan == 0, left, same)
-    last = jnp.where(chan == devices - 1, right, same)
-    pos = jnp.concatenate([first, same, last], axis=0)
-    hot = (pos[:, :, None] == jnp.arange(slots + REACH, dtype=jnp.int32)).astype(BF16)
-    return jnp.stack(send_pos), hot
+    return pl.pallas_call(
+        functools.partial(link_kernel, regions),
+        out_shape=(
+            jax.ShapeDtypeStruct((2, slots), jnp.int32),
+            jax.ShapeDtypeStruct((27, slots, slots + REACH), BF16),
+        ),
+        in_specs=[SMEM, VMEM, pl.BlockSpec(memory_space=pl.ANY)],
+        out_specs=(VMEM, VMEM),
+        compiler_params=params(),
+        name="links",
+    )(jnp.stack([region, chan]), adjacency.T, before)
 
 
 def send_faces(faces, regions, devices):
@@ -664,12 +681,9 @@
         point_feats, order.reshape(square), keys.reshape(square), region, regions, cells
     )
     mine = pack(taps, down, middle)
-    late = mine[16, 0, 128] != 0
     theirs = [swap(mine, flip, devices) for flip in (1, 2, 3)]
     even, odd, down = prepare(me, mine, theirs, down_weight.shape[0])
-    adjacency = jnp.where(late, 0, adjacency)
-
-    send_pos, hot = links(adjacency, region, regions, chan, devices)
+    send_pos, hot = links(adjacency, region, regions, chan, middle)
     far = far_voxels(me, chunks, regions, slots, (down, hot, send_pos))
     from_two = swap(far, 2, devices)
     near_three, near_one, near, *faces = near_voxels(me, chunks, regions, far, send_pos, slots)

time: 82.1 us -> 81.4 us (level)
  starting transfers between devices: 27.8 us -> 32.4 us
  waiting for transfers between devices: 9.22 us -> 6.47 us
  other arithmetic: 9.16 us -> 7.52 us
  Pallas kernels: 31.4 us -> 32.8 us
  local copies, waits for them, and re-layouts: 2 us -> 1.08 us
    ppermute x10, waiting for transfers between devices: 6.84 us -> 3.75 us  [swap(): lax.ppermute(value, 'chan', [(source, source ^ flip) for source in range(...]
    ppermute x10, starting transfers between devices: 8.87 us -> 11.9 us  [swap(): lax.ppermute(value, 'chan', [(source, source ^ flip) for source in range(...]
    ppermute x7, starting transfers between devices: 13.6 us -> 16 us  [send(): lax.ppermute(value, 'region', pair)]
    pallas_call x0 -> x1, Pallas kernels: none -> 1.18 us  [links(): pl.pallas_call(functools.partial(link_kernel, regions), out_shape=(jax.Sh...]
    ppermute x4, starting transfers between devices: 5.37 us -> 4.41 us  [send_faces(): got.append(lax.ppermute(faces[flip], ('region', 'chan'), pairs))]
    reduce_sum x3 -> x0, other arithmetic: 0.84 us -> none  [the longest x2 0.73 us: links(): jnp.sum((member[None, None, :] & (every < there[:, :, None])).astype(jnp....]
  transfers between devices with their start and end apart: 21 -> 21, of which waited for: 6 -> 6; matrix products, arithmetic and copies ran while one was open for 3% -> 0% of each run, Pallas kernels for 22% -> 21%
where the time goes in v1:
time: 81.4 us; the launch traced here: 81.2 us
  Pallas kernels  32.8 us (40%)
  starting transfers between devices  32.4 us (40%)
  other arithmetic  7.52 us (9%)
  waiting for transfers between devices  6.47 us (8%)
  local copies, waits for them, and re-layouts  1.08 us (1%)
  between operations  0.95 us (1%)
    ppermute x7, starting transfers between devices, send(): lax.ppermute(value, 'region', pair)  16 us
    ppermute x10, starting transfers between devices, swap(): lax.ppermute(value, 'chan', [(source, source ^ flip) for source in range(...  11.9 us
    pallas_call x3, Pallas kernels, permute_piece(): pl.pallas_call(functools.partial(piece_kernel, depth, cells, flips), out_...  9.67 us
    sort x1, other arithmetic, body(): lax.sort((destination * cells + code, jnp.arange(points, dtype=jnp.int32)...  6.45 us
    pallas_call x1, Pallas kernels, near_voxels(): pl.pallas_call(functools.partial(near_kernel, slots, len(chunks)), out_sh...  5.37 us
    pallas_call x1, Pallas kernels, far_voxels(): pl.pallas_call(functools.partial(far_kernel, len(chunks)), out_shape=jax....  4.86 us
    ppermute x4, starting transfers between devices, send_faces(): got.append(lax.ppermute(faces[flip], ('region', 'chan'), pairs))  4.41 us
    pallas_call x1, Pallas kernels, convolve(): pl.pallas_call(functools.partial(odd_kernel, slots), out_shape=[jax.Shape...  4.31 us
  transfers between devices with their start and end apart: 21, of which 6 were waited for; matrix products, arithmetic and copies ran while one was open for 0% of the time, Pallas kernels for 21%

profile of v1, /device:TPU:0, one launch (start us, length us, event | category | flops | bytes accessed | tf_op | source)
XLA Modules:
  0.0 81.2 jit_solution(16091516727983859324)
XLA Ops:
  0.0 1.0 %fusion.4 = s32[16384]{0:T(1024)S(1)} fusion(s32[16384]{0:T(1024)} %param.10, s32[16384]{0:T(1024)} %param.11), kind=kLoop, calls=%fused_computation.14 | loop fusion | flops 720896 | bytes 196608 | tf_op jit(solution)/shard_map/add | solution.py:675
  1.0 6.4 %sort.15 = (s32[16384]{0:T(1024)S(1)}, s32[16384]{0:T(1024)S(1)}) sort(s32[16384]{0:T(1024)S(1)} %fusion.4, s32[16384]{0:T(1024)S(1)} %iota.3), dimensions={0}, to_apply=%region_0.1 | sort | flops 229376 | bytes 262144 | tf_op jit(solution)/shard_map/sort | solution.py:674
  7.5 0.0 copy-start.3
  7.5 1.0 %copy-done.3 = bf16[16,16384]{1,0:T(8,128)(2,1)S(1)} copy-done((bf16[16,16384]{1,0:T(8,128)(2,1)S(1)}, bf16[16,16384]{1,0:T(8,128)(2,1)}, u32[]{:S(2)}) %copy-start.3) | copy-done | bytes 524312
  8.5 2.4 %permute_piece.3 = (bf16[18,16,128]{2,1,0:T(8,128)(2,1)S(1)}, bf16[18,16,128]{2,1,0:T(8,128)(2,1)S(1)}) custom-call(s32[1]{0:T(128)} %bitcast.1.region, bf16[16,16384]{1,0:T(8,128)(2,1)S(1)} %copy-done.3, s32[128,128]{1,0:T(8,128)S(1)} %bitcast.17, s32[128,128]{1,0:T(8,128)S(1)} %bitcast.14), custom_call_target="tpu_custom_call" | custom-call | flops 2000000000 | bytes 1000000 | tf_op jit(solution)/shard_map/permute_piece/pallas_call | solution.py:132
  11.0 0.0 copy-start
  11.0 0.0 copy-start.1
  11.0 0.0 copy-start.2
  11.0 0.0 copy-start.4
  11.0 2.4 %permute_piece.4 = (bf16[18,16,128]{2,1,0:T(8,128)(2,1)S(1)}, bf16[18,16,128]{2,1,0:T(8,128)(2,1)S(1)}) custom-call(s32[1]{0:T(128)} %bitcast.1.region, bf16[16,16384]{1,0:T(8,128)(2,1)S(1)} %copy-done.3, s32[128,128]{1,0:T(8,128)S(1)} %bitcast.18, s32[128,128]{1,0:T(8,128)S(1)} %bitcast.15, bf16[18,16,128]{2,1,0:T(8,128)(2,1)S(1)} %get-tuple-element.33.rest_0_), custom_call_target="tpu_custom_call" | custom-call | flops 2000000000 | bytes 1000000 | tf_op jit(solution)/shard_map/permute_piece/pallas_call | solution.py:132
  13.5 0.1 pack.1.own
  13.6 0.5 collective-permute-start.7
  14.1 2.6 %collective-permute-start.8 = (bf16[17,16,192]{2,1,0:T(8,128)(2,1)S(1)}, bf16[17,16,192]{2,1,0:T(8,128)(2,1)S(1)}, u32[]{:S(2)}, u32[]{:S(2)}) collective-permute-start(bf16[17,16,192]{2,1,0:T(8,128)(2,1)S(1)} %pack.1.own), channel_id=1, source_target_pairs={{0,2},{1,3},{2,0},{3,1},{4,6},{5,7},{6,4},{7,5},{8,10},{9,11},{10,... | collective-permute-start | bytes 313352 | tf_op jit(solution)/shard_map/ppermute | solution.py:658
  16.7 0.1 collective-permute-start.9
  16.7 3.8 %collective-permute-start = (bf16[18,16,128]{2,1,0:T(8,128)(2,1)S(1)}, bf16[18,16,128]{2,1,0:T(8,128)(2,1)S(1)}, u32[]{:S(2)}, u32[]{:S(2)}) collective-permute-start(bf16[18,16,128]{2,1,0:T(8,128)(2,1)S(1)} %get-tuple-element.33.rest_0_), channel_id=1, source_target_pairs={{0,24},{4,28},{8,16},{12,20},{16,8},{20,12},{24,0},{28,4},{1,25},{... | collective-permute-start | bytes 221192 | tf_op jit(solution)/shard_map/ppermute | solution.py:152
  20.5 1.2 %collective-permute-start.1 = (bf16[18,16,128]{2,1,0:T(8,128)(2,1)S(1)}, bf16[18,16,128]{2,1,0:T(8,128)(2,1)S(1)}, u32[]{:S(2)}, u32[]{:S(2)}) collective-permute-start(bf16[18,16,128]{2,1,0:T(8,128)(2,1)S(1)} %get-tuple-element.34), channel_id=1, source_target_pairs={{0,28},{4,24},{8,20},{12,16},{16,12},{20,8},{24,4},{28,0},{1,29},{... | collective-permute-start | bytes 221192 | tf_op jit(solution)/shard_map/ppermute | solution.py:152
  21.7 0.1 pad_add_fusion.place_of
  21.8 1.2 %links.1 = (s32[2,64]{1,0:T(2,128)S(1)}, bf16[27,64,80]{2,1,0:T(8,128)(2,1)S(1)}) custom-call(s32[2]{0:T(128)S(1)} %pad_add_fusion.place_of, s32[26,64]{1,0:T(8,128)S(1)} %bitcast.13, bf16[18,16,128]{2,1,0:T(8,128)(2,1)S(1)} %get-tuple-element.35.rest_0_._), custom_call_target="tpu_custom_call" | custom-call | tf_op jit(solution)/shard_map/links/pallas_call | solution.py:634
  23.0 0.5 collective-permute-done.rest_1_.rest_0_
  23.4 5.1 %collective-permute-start.2 = (bf16[18,16,128]{2,1,0:T(8,128)(2,1)S(1)}, bf16[18,16,128]{2,1,0:T(8,128)(2,1)S(1)}, u32[]{:S(2)}, u32[]{:S(2)}) collective-permute-start(bf16[18,16,128]{2,1,0:T(8,128)(2,1)S(1)} %get-tuple-element.35.rest_0_._), channel_id=1, source_target_pairs={{0,16},{4,20},{8,24},{12,28},{16,0},{20,4},{24,8},{28,12},{1,17},{... | collective-permute-start | bytes 221192 | tf_op jit(solution)/shard_map/ppermute | solution.py:152
  28.5 0.0 collective-permute-done.1.rest_2_.rest_1_
  28.5 2.5 %collective-permute-start.3 = (bf16[18,16,128]{2,1,0:T(8,128)(2,1)S(1)}, bf16[18,16,128]{2,1,0:T(8,128)(2,1)S(1)}, u32[]{:S(2)}, u32[]{:S(2)}) collective-permute-start(bf16[18,16,128]{2,1,0:T(8,128)(2,1)S(1)} %get-tuple-element.36), channel_id=1, source_target_pairs={{0,20},{4,16},{8,28},{12,24},{16,4},{20,0},{24,12},{28,8},{1,21},{... | collective-permute-start | bytes 221192 | tf_op jit(solution)/shard_map/ppermute | solution.py:152
  31.0 0.0 copy-done.4
  31.0 4.8 %permute_piece.5 = (bf16[18,16,128]{2,1,0:T(8,128)(2,1)S(1)}, bf16[18,16,128]{2,1,0:T(8,128)(2,1)S(1)}, bf16[18,16,128]{2,1,0:T(8,128)(2,1)S(1)}, bf16[18,16,128]{2,1,0:T(8,128)(2,1)S(1)}) custom-call(s32[1]{0:T(128)} %bitcast.1.region, bf16[16,16384]{1,0:T(8,128)(2,1)S(1)} %copy-done.4, s32[128,128]{1,0:T(8,128)S(1)} %bitcast.19, s32[128,128]{1,0:T(8,128)S(1)} %bitcast.16, ...), custom_call_target="tpu_custom_call" | custom-call | flops 2000000000 | bytes 1000000 | tf_op jit(solution)/shard_map/permute_piece/pallas_call | solution.py:132
  35.8 0.0 collective-permute-done.7.one
  35.8 0.1 collective-permute-start.4
  35.9 0.0 collective-permute-done.8.two
  35.9 2.9 %collective-permute-start.5 = (bf16[18,16,128]{2,1,0:T(8,128)(2,1)S(1)}, bf16[18,16,128]{2,1,0:T(8,128)(2,1)S(1)}, u32[]{:S(2)}, u32[]{:S(2)}) collective-permute-start(bf16[18,16,128]{2,1,0:T(8,128)(2,1)S(1)} %get-tuple-element.38), channel_id=1, source_target_pairs={{0,12},{4,8},{8,4},{12,0},{16,28},{20,24},{24,20},{28,16},{1,13},{... | collective-permute-start | bytes 221192 | tf_op jit(solution)/shard_map/ppermute | solution.py:152
  38.8 0.0 collective-permute-done.9.three
  38.8 0.6 collective-permute-start.6
  39.3 1.5 %prepare.1 = (bf16[2,9,256,256]{3,2,1,0:T(8,128)(2,1)S(1)}, bf16[2,9,256,256]{3,2,1,0:T(8,128)(2,1)S(1)}, bf16[128,512]{1,0:T(8,128)(2,1)S(1)}) custom-call(s32[1]{0:T(128)} %bitcast.chan, bf16[17,16,192]{2,1,0:T(8,128)(2,1)S(1)} %pack.1.own, bf16[17,16,192]{2,1,0:T(8,128)(2,1)S(1)} %collective-permute-done.7.one, ...), custom_call_target="tpu_custom_call" | custom-call | flops 2000000000 | bytes 3000000 | tf_op jit(solution)/shard_map/prepare/pallas_call | solution.py:429
  40.9 0.0 collective-permute-done.2.rest_2_
  40.9 0.0 collective-permute-done.3.rest_3_
  40.9 0.0 collective-permute-done.4.rest_4_
  40.9 1.0 %collective-permute-done.5.rest_5_ = bf16[18,16,128]{2,1,0:T(8,128)(2,1)S(1)} collective-permute-done((bf16[18,16,128]{2,1,0:T(8,128)(2,1)S(1)}, bf16[18,16,128]{2,1,0:T(8,128)(2,1)S(1)}, u32[]{:S(2)}, u32[]{:S(2)}) %collective-permute-start.5) | collective-permute-done | bytes 73760 | tf_op jit(solution)/shard_map/ppermute | solution.py:152
  41.9 1.2 %collective-permute-done.6.rest_6_ = bf16[18,16,128]{2,1,0:T(8,128)(2,1)S(1)} collective-permute-done((bf16[18,16,128]{2,1,0:T(8,128)(2,1)S(1)}, bf16[18,16,128]{2,1,0:T(8,128)(2,1)S(1)}, u32[]{:S(2)}, u32[]{:S(2)}) %collective-permute-start.6) | collective-permute-done | bytes 73760 | tf_op jit(solution)/shard_map/ppermute | solution.py:152
  43.1 4.9 %far_voxels.1.rest_8_ = bf16[4,512,128]{2,1,0:T(8,128)(2,1)S(1)} custom-call(s32[1]{0:T(128)} %bitcast.chan, bf16[18,16,128]{2,1,0:T(8,128)(2,1)S(1)} %collective-permute-done.rest_1_.rest_0_, bf16[18,16,128]{2,1,0:T(8,128)(2,1)S(1)} %collective-permute-done.1.rest_2_.rest_1_, bf16[18,16,128]{2,1,0:T(8,128)(2,1)S(1)} %collective-permute-done.2.rest_2_, ...), custom_call_target="tpu_custom_call" | custom-call | flops 4000000000 | bytes 1200000 | tf_op jit(solution)/shard_map/far_voxels/pallas_call | solution.py:327
  48.0 0.0 copy-start.5
  48.0 1.6 %collective-permute-start.12 = (bf16[4,512,128]{2,1,0:T(8,128)(2,1)S(1)}, bf16[4,512,128]{2,1,0:T(8,128)(2,1)S(1)}, u32[]{:S(2)}, u32[]{:S(2)}) collective-permute-start(bf16[4,512,128]{2,1,0:T(8,128)(2,1)S(1)} %far_voxels.1.rest_8_), channel_id=1, source_target_pairs={{0,2},{1,3},{2,0},{3,1},{4,6},{5,7},{6,4},{7,5},{8,10},{9,11},{10,... | collective-permute-start | bytes 1572872 | tf_op jit(solution)/shard_map/ppermute | solution.py:658
  49.6 5.4 %near_voxels.1 = (bf16[2,512,128]{2,1,0:T(8,128)(2,1)S(1)}, bf16[4,512,128]{2,1,0:T(8,128)(2,1)S(1)}, bf16[4,512,128]{2,1,0:T(8,128)(2,1)S(1)}, bf16[8,16,128]{2...) custom-call(s32[1]{0:T(128)} %bitcast.chan, ...), custom_call_target="tpu_custom_call" | custom-call | flops 4000000000 | bytes 3000000 | tf_op jit(solution)/shard_map/near_voxels/pallas_call | solution.py:340
  55.0 0.1 collective-permute-start.10
  55.1 2.4 %collective-permute-start.16 = (bf16[8,16,128]{2,1,0:T(8,128)(2,1)S(1)}, bf16[8,16,128]{2,1,0:T(8,128)(2,1)S(1)}, u32[]{:S(2)}, u32[]{:S(2)}) collective-permute-start(bf16[8,16,128]{2,1,0:T(8,128)(2,1)S(1)} %get-tuple-element.50), channel_id=1, source_target_pairs={{0,4},{4,8},{8,12},{12,16},{16,20},{20,24},{24,28},{7,3},{11,7},{1... | collective-permute-start | bytes 98312 | tf_op jit(solution)/shard_map/ppermute | solution.py:653
  57.5 0.7 collective-permute-start.17
  58.8 0.1 collective-permute-start.11
  59.0 0.1 collective-permute-done.12.planes.two
  59.1 0.7 collective-permute-start.14
  59.8 0.0 collective-permute-done.16.r0
  59.8 0.7 collective-permute-start.15
  60.5 0.0 collective-permute-done.17.r2
  60.5 5.0 %collective-permute-start.13 = (bf16[2,512,128]{2,1,0:T(8,128)(2,1)S(1)}, bf16[2,512,128]{2,1,0:T(8,128)(2,1)S(1)}, u32[]{:S(2)}, u32[]{:S(2)}) collective-permute-start(bf16[2,512,128]{2,1,0:T(8,128)(2,1)S(1)} %shared_planes.1), channel_id=1, source_target_pairs={{0,1},{1,0},{2,3},{3,2},{4,5},{5,4},{6,7},{7,6},{8,9},{9,8},{10,11... | collective-permute-start | bytes 786440 | tf_op jit(solution)/shard_map/ppermute | solution.py:658
  65.5 3.9 %even_sums.1.sums = f32[2,2,512,256]{3,2,1,0:T(8,128)S(1)} custom-call(bf16[4,512,128]{2,1,0:T(8,128)(2,1)S(1)} %get-tuple-element.49.own, bf16[4,512,128]{2,1,0:T(8,128)(2,1)S(1)} %collective-permute-done.12.planes.two, bf16[8,16,128]{2,1,0:T(8,128)(2,1)S(1)} %collective-permute-done.16.r0, bf16[8,16,128]{2,1,0:T(8,128)(2,1)S(1)} %collective-permute-done.17.r2, ...), custom_call_target="tpu_custom_call" | custom-call | flops 4000000000 | bytes 5000000 | tf_op jit(solution)/shard_map/even_sums/pallas_call | solution.py:536
  69.4 0.0 collective-permute-done.14.r1
  69.4 0.0 collective-permute-done.15.r3
  69.4 0.0 collective-permute-done.11.direct
  69.4 0.0 collective-permute-done.10.one
  69.4 0.0 collective-permute-done.13.passed
  69.5 4.3 %convolve.1 = (bf16[32,1024]{1,0:T(8,128)(2,1)S(1)}, bf16[32,1024]{1,0:T(8,128)(2,1)S(1)}, bf16[32,1024]{1,0:T(8,128)(2,1)S(1)}, bf16[32,1024]{1,0:T(8,128)(2,1)S(1)}) custom-call(s32[1]{0:T(128)} %bitcast.chan, s32[1]{0:T(128)S(6)} %copy.10.active, bf16[4,512,128]{2,1,0:T(8,128)(2,1)S(1)} %collective-permute-done.10.one, ...), custom_call_target="tpu_custom_call" | custom-call | flops 4000000000 | bytes 5000000 | tf_op jit(solution)/shard_map/convolve/pallas_call | solution.py:555
  73.8 0.1 collective-permute-start.18
  73.9 0.8 collective-permute-start.19
  74.7 1.1 %collective-permute-start.20 = (bf16[32,1024]{1,0:T(8,128)(2,1)S(1)}, bf16[32,1024]{1,0:T(8,128)(2,1)S(1)}, u32[]{:S(2)}, u32[]{:S(2)}) collective-permute-start(bf16[32,1024]{1,0:T(8,128)(2,1)S(1)} %get-tuple-element.56), channel_id=1, source_target_pairs={{0,3},{1,2},{2,1},{3,0},{4,7},{5,6},{6,5},{7,4},{8,11},{9,10},{10,... | collective-permute-start | bytes 196616 | tf_op jit(solution)/shard_map/ppermute | solution.py:658
  75.7 0.0 collective-permute-done.18.one
  75.7 3.1 %collective-permute-done.19.two = bf16[32,1024]{1,0:T(8,128)(2,1)S(1)} collective-permute-done((bf16[32,1024]{1,0:T(8,128)(2,1)S(1)}, bf16[32,1024]{1,0:T(8,128)(2,1)S(1)}, u32[]{:S(2)}, u32[]{:S(2)}) %collective-permute-start.19) | collective-permute-done | bytes 65568 | tf_op jit(solution)/shard_map/ppermute | solution.py:658
  78.8 0.5 collective-permute-done.20.three
  79.3 1.9 %finish.1 = bf16[64,2048]{1,0:T(8,128)(2,1)} custom-call(s32[1]{0:T(128)} %bitcast.chan, bf16[32,1024]{1,0:T(8,128)(2,1)S(1)} %get-tuple-element.53.own, bf16[32,1024]{1,0:T(8,128)(2,1)S(1)} %collective-permute-done.18.one, bf16[32,1024]{1,0:T(8,128)(2,1)S(1)} %collective-permute-done.19.two, bf16[32,1024]{1,0:T(8,128)(2,1)S(1)} %collective-permute-done.20.three), custom_call_target="tpu_custom_call" | custom-call | tf_op jit(solution)/shard_map/finish/pallas_call | solution.py:586
  (6 shorter events, 0.0 us)
Async XLA Ops:
  7.5 1.0 %copy-start.3 = (bf16[16,16384]{1,0:T(8,128)(2,1)S(1)}, bf16[16,16384]{1,0:T(8,128)(2,1)}, u32[]{:S(2)}) copy-start(bf16[16,16384]{1,0:T(8,128)(2,1)} %feats.5) | copy-start | bytes 1572868
  11.0 2.5 %copy-start = (bf16[16,64,3,3,3]{1,0,4,3,2:T(8,128)(2,1)S(1)}, bf16[16,64,3,3,3]{1,0,4,3,2:T(8,128)(2,1)}, u32[]{:S(2)}) copy-start(bf16[16,64,3,3,3]{1,0,4,3,2:T(8,128)(2,1)} %param.14) | copy-start | bytes 165892
  11.0 2.5 %copy-start.1 = (bf16[128,16,2,2,2]{0,4,3,2,1:T(2,128)(2,1)S(1)}, bf16[128,16,2,2,2]{0,4,3,2,1:T(2,128)(2,1)}, u32[]{:S(2)}) copy-start(bf16[128,16,2,2,2]{0,4,3,2,1:T(2,128)(2,1)} %param.15) | copy-start | bytes 98308
  11.0 10.8 %copy-start.2 = (s32[64,26]{0,1:T(8,128)S(1)}, s32[64,26]{0,1:T(8,128)}, u32[]{:S(2)}) copy-start(s32[64,26]{0,1:T(8,128)} %param.12) | copy-start | bytes 19972
  11.0 20.0 %copy-start.4 = (bf16[16,16384]{1,0:T(8,128)(2,1)S(1)}, bf16[16,16384]{1,0:T(8,128)(2,1)}, u32[]{:S(2)}) copy-start(bf16[16,16384]{1,0:T(8,128)(2,1)} %feats.5) | copy-start | bytes 1572868
  13.6 22.2 %collective-permute-start.7 = (bf16[17,16,192]{2,1,0:T(8,128)(2,1)S(1)}, bf16[17,16,192]{2,1,0:T(8,128)(2,1)S(1)}, u32[]{:S(2)}, u32[]{:S(2)}) collective-permute-start(bf16[17,16,192]{2,1,0:T(8,128)(2,1)S(1)} %pack.1.own), channel_id=1, source_target_pairs={{0,1},{1,0},{2,3},{3,2},{4,5},{5,4},{6,7},{7,6},{8,9},{9,8},{10,11... | collective-permute-start | bytes 313352 | tf_op jit(solution)/shard_map/ppermute | solution.py:658
  14.1 21.8 %collective-permute-start.8 = (bf16[17,16,192]{2,1,0:T(8,128)(2,1)S(1)}, bf16[17,16,192]{2,1,0:T(8,128)(2,1)S(1)}, u32[]{:S(2)}, u32[]{:S(2)}) collective-permute-start(bf16[17,16,192]{2,1,0:T(8,128)(2,1)S(1)} %pack.1.own), channel_id=1, source_target_pairs={{0,2},{1,3},{2,0},{3,1},{4,6},{5,7},{6,4},{7,5},{8,10},{9,11},{10,... | collective-permute-start | bytes 313352 | tf_op jit(solution)/shard_map/ppermute | solution.py:658
  16.7 22.1 %collective-permute-start.9 = (bf16[17,16,192]{2,1,0:T(8,128)(2,1)S(1)}, bf16[17,16,192]{2,1,0:T(8,128)(2,1)S(1)}, u32[]{:S(2)}, u32[]{:S(2)}) collective-permute-start(bf16[17,16,192]{2,1,0:T(8,128)(2,1)S(1)} %pack.1.own), channel_id=1, source_target_pairs={{0,3},{1,2},{2,1},{3,0},{4,7},{5,6},{6,5},{7,4},{8,11},{9,10},{10,... | collective-permute-start | bytes 313352 | tf_op jit(solution)/shard_map/ppermute | solution.py:658
  16.7 6.7 %collective-permute-start = (bf16[18,16,128]{2,1,0:T(8,128)(2,1)S(1)}, bf16[18,16,128]{2,1,0:T(8,128)(2,1)S(1)}, u32[]{:S(2)}, u32[]{:S(2)}) collective-permute-start(bf16[18,16,128]{2,1,0:T(8,128)(2,1)S(1)} %get-tuple-element.33.rest_0_), channel_id=1, source_target_pairs={{0,24},{4,28},{8,16},{12,20},{16,8},{20,12},{24,0},{28,4},{1,25},{... | collective-permute-start | bytes 221192 | tf_op jit(solution)/shard_map/ppermute | solution.py:152
  20.5 7.9 %collective-permute-start.1 = (bf16[18,16,128]{2,1,0:T(8,128)(2,1)S(1)}, bf16[18,16,128]{2,1,0:T(8,128)(2,1)S(1)}, u32[]{:S(2)}, u32[]{:S(2)}) collective-permute-start(bf16[18,16,128]{2,1,0:T(8,128)(2,1)S(1)} %get-tuple-element.34), channel_id=1, source_target_pairs={{0,28},{4,24},{8,20},{12,16},{16,12},{20,8},{24,4},{28,0},{1,29},{... | collective-permute-start | bytes 221192 | tf_op jit(solution)/shard_map/ppermute | solution.py:152
  23.4 17.4 %collective-permute-start.2 = (bf16[18,16,128]{2,1,0:T(8,128)(2,1)S(1)}, bf16[18,16,128]{2,1,0:T(8,128)(2,1)S(1)}, u32[]{:S(2)}, u32[]{:S(2)}) collective-permute-start(bf16[18,16,128]{2,1,0:T(8,128)(2,1)S(1)} %get-tuple-element.35.rest_0_._), channel_id=1, source_target_pairs={{0,16},{4,20},{8,24},{12,28},{16,0},{20,4},{24,8},{28,12},{1,17},{... | collective-permute-start | bytes 221192 | tf_op jit(solution)/shard_map/ppermute | solution.py:152
  28.5 12.4 %collective-permute-start.3 = (bf16[18,16,128]{2,1,0:T(8,128)(2,1)S(1)}, bf16[18,16,128]{2,1,0:T(8,128)(2,1)S(1)}, u32[]{:S(2)}, u32[]{:S(2)}) collective-permute-start(bf16[18,16,128]{2,1,0:T(8,128)(2,1)S(1)} %get-tuple-element.36), channel_id=1, source_target_pairs={{0,20},{4,16},{8,28},{12,24},{16,4},{20,0},{24,12},{28,8},{1,21},{... | collective-permute-start | bytes 221192 | tf_op jit(solution)/shard_map/ppermute | solution.py:152
  35.8 5.1 %collective-permute-start.4 = (bf16[18,16,128]{2,1,0:T(8,128)(2,1)S(1)}, bf16[18,16,128]{2,1,0:T(8,128)(2,1)S(1)}, u32[]{:S(2)}, u32[]{:S(2)}) collective-permute-start(bf16[18,16,128]{2,1,0:T(8,128)(2,1)S(1)} %get-tuple-element.37), channel_id=1, source_target_pairs={{0,8},{4,12},{8,0},{12,4},{16,24},{20,28},{24,16},{28,20},{1,9},{5... | collective-permute-start | bytes 221192 | tf_op jit(solution)/shard_map/ppermute | solution.py:152
  35.9 6.0 %collective-permute-start.5 = (bf16[18,16,128]{2,1,0:T(8,128)(2,1)S(1)}, bf16[18,16,128]{2,1,0:T(8,128)(2,1)S(1)}, u32[]{:S(2)}, u32[]{:S(2)}) collective-permute-start(bf16[18,16,128]{2,1,0:T(8,128)(2,1)S(1)} %get-tuple-element.38), channel_id=1, source_target_pairs={{0,12},{4,8},{8,4},{12,0},{16,28},{20,24},{24,20},{28,16},{1,13},{... | collective-permute-start | bytes 221192 | tf_op jit(solution)/shard_map/ppermute | solution.py:152
  38.8 4.4 %collective-permute-start.6 = (bf16[18,16,128]{2,1,0:T(8,128)(2,1)S(1)}, bf16[18,16,128]{2,1,0:T(8,128)(2,1)S(1)}, u32[]{:S(2)}, u32[]{:S(2)}) collective-permute-start(bf16[18,16,128]{2,1,0:T(8,128)(2,1)S(1)} %get-tuple-element.39), channel_id=1, source_target_pairs={{0,4},{4,0},{8,12},{12,8},{16,20},{20,16},{24,28},{28,24},{1,5},{5... | collective-permute-start | bytes 221192 | tf_op jit(solution)/shard_map/ppermute | solution.py:152
  48.0 17.5 %copy-start.5 = (bf16[256,128]{1,0:T(8,128)(2,1)S(1)}, bf16[256,128]{1,0:T(8,128)(2,1)}, u32[]{:S(2)}) copy-start(bf16[256,128]{1,0:T(8,128)(2,1)} %constant.64.clone.pick) | copy-start | bytes 196612
  48.0 11.1 %collective-permute-start.12 = (bf16[4,512,128]{2,1,0:T(8,128)(2,1)S(1)}, bf16[4,512,128]{2,1,0:T(8,128)(2,1)S(1)}, u32[]{:S(2)}, u32[]{:S(2)}) collective-permute-start(bf16[4,512,128]{2,1,0:T(8,128)(2,1)S(1)} %far_voxels.1.rest_8_), channel_id=1, source_target_pairs={{0,2},{1,3},{2,0},{3,1},{4,6},{5,7},{6,4},{7,5},{8,10},{9,11},{10,... | collective-permute-start | bytes 1572872 | tf_op jit(solution)/shard_map/ppermute | solution.py:658
  55.0 14.4 %collective-permute-start.10 = (bf16[4,512,128]{2,1,0:T(8,128)(2,1)S(1)}, bf16[4,512,128]{2,1,0:T(8,128)(2,1)S(1)}, u32[]{:S(2)}, u32[]{:S(2)}) collective-permute-start(bf16[4,512,128]{2,1,0:T(8,128)(2,1)S(1)} %get-tuple-element.44), channel_id=1, source_target_pairs={{0,1},{1,0},{2,3},{3,2},{4,5},{5,4},{6,7},{7,6},{8,9},{9,8},{10,11... | collective-permute-start | bytes 1572872 | tf_op jit(solution)/shard_map/ppermute | solution.py:658
  55.1 4.7 %collective-permute-start.16 = (bf16[8,16,128]{2,1,0:T(8,128)(2,1)S(1)}, bf16[8,16,128]{2,1,0:T(8,128)(2,1)S(1)}, u32[]{:S(2)}, u32[]{:S(2)}) collective-permute-start(bf16[8,16,128]{2,1,0:T(8,128)(2,1)S(1)} %get-tuple-element.50), channel_id=1, source_target_pairs={{0,4},{4,8},{8,12},{12,16},{16,20},{20,24},{24,28},{7,3},{11,7},{1... | collective-permute-start | bytes 98312 | tf_op jit(solution)/shard_map/ppermute | solution.py:653
  57.5 3.0 %collective-permute-start.17 = (bf16[8,16,128]{2,1,0:T(8,128)(2,1)S(1)}, bf16[8,16,128]{2,1,0:T(8,128)(2,1)S(1)}, u32[]{:S(2)}, u32[]{:S(2)}) collective-permute-start(bf16[8,16,128]{2,1,0:T(8,128)(2,1)S(1)} %get-tuple-element.51), channel_id=1, source_target_pairs={{2,4},{6,8},{10,12},{14,16},{18,20},{22,24},{26,28},{5,3},{9,7},{1... | collective-permute-start | bytes 98312 | tf_op jit(solution)/shard_map/ppermute | solution.py:653
  58.8 10.6 %collective-permute-start.11 = (bf16[2,512,128]{2,1,0:T(8,128)(2,1)S(1)}, bf16[2,512,128]{2,1,0:T(8,128)(2,1)S(1)}, u32[]{:S(2)}, u32[]{:S(2)}) collective-permute-start(bf16[2,512,128]{2,1,0:T(8,128)(2,1)S(1)} %get-tuple-element.45), channel_id=1, source_target_pairs={{0,3},{1,2},{2,1},{3,0},{4,7},{5,6},{6,5},{7,4},{8,11},{9,10},{10,... | collective-permute-start | bytes 786440 | tf_op jit(solution)/shard_map/ppermute | solution.py:658
  59.1 10.3 %collective-permute-start.14 = (bf16[8,16,128]{2,1,0:T(8,128)(2,1)S(1)}, bf16[8,16,128]{2,1,0:T(8,128)(2,1)S(1)}, u32[]{:S(2)}, u32[]{:S(2)}) collective-permute-start(bf16[8,16,128]{2,1,0:T(8,128)(2,1)S(1)} %get-tuple-element.46), channel_id=1, source_target_pairs={{1,4},{5,8},{9,12},{13,16},{17,20},{21,24},{25,28},{6,3},{10,7},{1... | collective-permute-start | bytes 98312 | tf_op jit(solution)/shard_map/ppermute | solution.py:653
  59.8 9.6 %collective-permute-start.15 = (bf16[8,16,128]{2,1,0:T(8,128)(2,1)S(1)}, bf16[8,16,128]{2,1,0:T(8,128)(2,1)S(1)}, u32[]{:S(2)}, u32[]{:S(2)}) collective-permute-start(bf16[8,16,128]{2,1,0:T(8,128)(2,1)S(1)} %get-tuple-element.47), channel_id=1, source_target_pairs={{3,4},{7,8},{11,12},{15,16},{19,20},{23,24},{27,28},{4,3},{8,7},{1... | collective-permute-start | bytes 98312 | tf_op jit(solution)/shard_map/ppermute | solution.py:653
  60.5 9.0 %collective-permute-start.13 = (bf16[2,512,128]{2,1,0:T(8,128)(2,1)S(1)}, bf16[2,512,128]{2,1,0:T(8,128)(2,1)S(1)}, u32[]{:S(2)}, u32[]{:S(2)}) collective-permute-start(bf16[2,512,128]{2,1,0:T(8,128)(2,1)S(1)} %shared_planes.1), channel_id=1, source_target_pairs={{0,1},{1,0},{2,3},{3,2},{4,5},{5,4},{6,7},{7,6},{8,9},{9,8},{10,11... | collective-permute-start | bytes 786440 | tf_op jit(solution)/shard_map/ppermute | solution.py:658
  73.8 1.9 %collective-permute-start.18 = (bf16[32,1024]{1,0:T(8,128)(2,1)S(1)}, bf16[32,1024]{1,0:T(8,128)(2,1)S(1)}, u32[]{:S(2)}, u32[]{:S(2)}) collective-permute-start(bf16[32,1024]{1,0:T(8,128)(2,1)S(1)} %get-tuple-element.54), channel_id=1, source_target_pairs={{0,1},{1,0},{2,3},{3,2},{4,5},{5,4},{6,7},{7,6},{8,9},{9,8},{10,11... | collective-permute-start | bytes 196616 | tf_op jit(solution)/shard_map/ppermute | solution.py:658
  73.9 4.9 %collective-permute-start.19 = (bf16[32,1024]{1,0:T(8,128)(2,1)S(1)}, bf16[32,1024]{1,0:T(8,128)(2,1)S(1)}, u32[]{:S(2)}, u32[]{:S(2)}) collective-permute-start(bf16[32,1024]{1,0:T(8,128)(2,1)S(1)} %get-tuple-element.55), channel_id=1, source_target_pairs={{0,2},{1,3},{2,0},{3,1},{4,6},{5,7},{6,4},{7,5},{8,10},{9,11},{10,... | collective-permute-start | bytes 196616 | tf_op jit(solution)/shard_map/ppermute | solution.py:658
  74.7 4.7 %collective-permute-start.20 = (bf16[32,1024]{1,0:T(8,128)(2,1)S(1)}, bf16[32,1024]{1,0:T(8,128)(2,1)S(1)}, u32[]{:S(2)}, u32[]{:S(2)}) collective-permute-start(bf16[32,1024]{1,0:T(8,128)(2,1)S(1)} %get-tuple-element.56), channel_id=1, source_target_pairs={{0,3},{1,2},{2,1},{3,0},{4,7},{5,6},{6,5},{7,4},{8,11},{9,10},{10,... | collective-permute-start | bytes 196616 | tf_op jit(solution)/shard_map/ppermute | solution.py:658

commit v2 on v1

--- a/solution.py
+++ b/solution.py
@@ -684,7 +684,7 @@
     theirs = [swap(mine, flip, devices) for flip in (1, 2, 3)]
     even, odd, down = prepare(me, mine, theirs, down_weight.shape[0])
     send_pos, hot = links(adjacency, region, regions, chan, middle)
-    far = far_voxels(me, chunks, regions, slots, (down, hot, send_pos))
+    far = far_voxels(me, chunks, regions, slots, (hot, send_pos, *theirs))
     from_two = swap(far, 2, devices)
     near_three, near_one, near, *faces = near_voxels(me, chunks, regions, far, send_pos, slots)
     from_three = swap(near_three, 3, devices)

time: 81.4 us -> 80.3 us (0.986)
  starting transfers between devices: 32.4 us -> 29.3 us
  waiting for transfers between devices: 6.47 us -> 8.38 us
    ppermute x7, starting transfers between devices: 16 us -> 11.7 us  [send(): lax.ppermute(value, 'region', pair)]
    ppermute x7, waiting for transfers between devices: 2.71 us -> 4.38 us  [send(): lax.ppermute(value, 'region', pair)]
    ppermute x4, starting transfers between devices: 4.41 us -> 5.65 us  [send_faces(): got.append(lax.ppermute(faces[flip], ('region', 'chan'), pairs))]
  transfers between devices with their start and end apart: 21 -> 21, of which waited for: 6 -> 6; matrix products, arithmetic and copies ran while one was open for 0% -> 0% of each run, Pallas kernels for 21% -> 24%
where the time goes in v2:
time: 80.3 us; the launch traced here: 80 us
  Pallas kernels  32.8 us (41%)
  starting transfers between devices  29.3 us (36%)
  waiting for transfers between devices  8.38 us (10%)
  other arithmetic  7.52 us (9%)
  local copies, waits for them, and re-layouts  1.07 us (1%)
  between operations  0.92 us (1%)
    ppermute x10, starting transfers between devices, swap(): lax.ppermute(value, 'chan', [(source, source ^ flip) for source in range(...  11.9 us
    ppermute x7, starting transfers between devices, send(): lax.ppermute(value, 'region', pair)  11.7 us
    pallas_call x3, Pallas kernels, permute_piece(): pl.pallas_call(functools.partial(piece_kernel, depth, cells, flips), out_...  9.67 us
    sort x1, other arithmetic, body(): lax.sort((destination * cells + code, jnp.arange(points, dtype=jnp.int32)...  6.45 us
    ppermute x4, starting transfers between devices, send_faces(): got.append(lax.ppermute(faces[flip], ('region', 'chan'), pairs))  5.65 us
    pallas_call x1, Pallas kernels, near_voxels(): pl.pallas_call(functools.partial(near_kernel, slots, len(chunks)), out_sh...  5.37 us
    pallas_call x1, Pallas kernels, far_voxels(): pl.pallas_call(functools.partial(far_kernel, len(chunks)), out_shape=jax....  4.86 us
    ppermute x7, waiting for transfers between devices, send(): lax.ppermute(value, 'region', pair)  4.38 us
  transfers between devices with their start and end apart: 21, of which 6 were waited for; matrix products, arithmetic and copies ran while one was open for 0% of the time, Pallas kernels for 24%

profile of v2, /device:TPU:0, one launch (start us, length us, event | category | flops | bytes accessed | tf_op | source)
XLA Modules:
  0.0 80.0 jit_solution(4160249187750731901)
XLA Ops:
  0.0 1.0 %fusion.4 = s32[16384]{0:T(1024)S(1)} fusion(s32[16384]{0:T(1024)} %param.10, s32[16384]{0:T(1024)} %param.11), kind=kLoop, calls=%fused_computation.14 | loop fusion | flops 720896 | bytes 196608 | tf_op jit(solution)/shard_map/add | solution.py:675
  1.0 6.4 %sort.15 = (s32[16384]{0:T(1024)S(1)}, s32[16384]{0:T(1024)S(1)}) sort(s32[16384]{0:T(1024)S(1)} %fusion.4, s32[16384]{0:T(1024)S(1)} %iota.3), dimensions={0}, to_apply=%region_0.1 | sort | flops 229376 | bytes 262144 | tf_op jit(solution)/shard_map/sort | solution.py:674
  7.5 0.0 copy-start.3
  7.5 1.0 %copy-done.3 = bf16[16,16384]{1,0:T(8,128)(2,1)S(1)} copy-done((bf16[16,16384]{1,0:T(8,128)(2,1)S(1)}, bf16[16,16384]{1,0:T(8,128)(2,1)}, u32[]{:S(2)}) %copy-start.3) | copy-done | bytes 524312
  8.5 2.4 %permute_piece.3 = (bf16[18,16,128]{2,1,0:T(8,128)(2,1)S(1)}, bf16[18,16,128]{2,1,0:T(8,128)(2,1)S(1)}) custom-call(s32[1]{0:T(128)} %bitcast.1.region, bf16[16,16384]{1,0:T(8,128)(2,1)S(1)} %copy-done.3, s32[128,128]{1,0:T(8,128)S(1)} %bitcast.17, s32[128,128]{1,0:T(8,128)S(1)} %bitcast.14), custom_call_target="tpu_custom_call" | custom-call | flops 2000000000 | bytes 1000000 | tf_op jit(solution)/shard_map/permute_piece/pallas_call | solution.py:132
  11.0 5.1 %collective-permute-start = (bf16[18,16,128]{2,1,0:T(8,128)(2,1)S(1)}, bf16[18,16,128]{2,1,0:T(8,128)(2,1)S(1)}, u32[]{:S(2)}, u32[]{:S(2)}) collective-permute-start(bf16[18,16,128]{2,1,0:T(8,128)(2,1)S(1)} %get-tuple-element.33.rest_0_), channel_id=1, source_target_pairs={{0,24},{4,28},{8,16},{12,20},{16,8},{20,12},{24,0},{28,4},{1,25},{... | collective-permute-start | bytes 221192 | tf_op jit(solution)/shard_map/ppermute | solution.py:152
  16.1 1.2 %collective-permute-start.1 = (bf16[18,16,128]{2,1,0:T(8,128)(2,1)S(1)}, bf16[18,16,128]{2,1,0:T(8,128)(2,1)S(1)}, u32[]{:S(2)}, u32[]{:S(2)}) collective-permute-start(bf16[18,16,128]{2,1,0:T(8,128)(2,1)S(1)} %get-tuple-element.34), channel_id=1, source_target_pairs={{0,28},{4,24},{8,20},{12,16},{16,12},{20,8},{24,4},{28,0},{1,29},{... | collective-permute-start | bytes 221192 | tf_op jit(solution)/shard_map/ppermute | solution.py:152
  17.2 2.4 %permute_piece.4 = (bf16[18,16,128]{2,1,0:T(8,128)(2,1)S(1)}, bf16[18,16,128]{2,1,0:T(8,128)(2,1)S(1)}) custom-call(s32[1]{0:T(128)} %bitcast.1.region, bf16[16,16384]{1,0:T(8,128)(2,1)S(1)} %copy-done.3, s32[128,128]{1,0:T(8,128)S(1)} %bitcast.18, s32[128,128]{1,0:T(8,128)S(1)} %bitcast.15, bf16[18,16,128]{2,1,0:T(8,128)(2,1)S(1)} %get-tuple-element.33.rest_0_), custom_call_target="tpu_custom_call" | custom-call | flops 2000000000 | bytes 1000000 | tf_op jit(solution)/shard_map/permute_piece/pallas_call | solution.py:132
  19.7 0.0 copy-done
  19.7 0.0 copy-done.1
  19.7 0.1 pack.1.own
  19.8 0.1 collective-permute-start.7
  19.8 1.6 %collective-permute-start.8 = (bf16[17,16,192]{2,1,0:T(8,128)(2,1)S(1)}, bf16[17,16,192]{2,1,0:T(8,128)(2,1)S(1)}, u32[]{:S(2)}, u32[]{:S(2)}) collective-permute-start(bf16[17,16,192]{2,1,0:T(8,128)(2,1)S(1)} %pack.1.own), channel_id=1, source_target_pairs={{0,2},{1,3},{2,0},{3,1},{4,6},{5,7},{6,4},{7,5},{8,10},{9,11},{10,... | collective-permute-start | bytes 313352 | tf_op jit(solution)/shard_map/ppermute | solution.py:658
  21.4 0.3 collective-permute-start.9
  22.4 0.0 collective-permute-done.rest_1_.rest_0_
  22.4 1.0 %collective-permute-start.2 = (bf16[18,16,128]{2,1,0:T(8,128)(2,1)S(1)}, bf16[18,16,128]{2,1,0:T(8,128)(2,1)S(1)}, u32[]{:S(2)}, u32[]{:S(2)}) collective-permute-start(bf16[18,16,128]{2,1,0:T(8,128)(2,1)S(1)} %get-tuple-element.35.rest_0_._), channel_id=1, source_target_pairs={{0,16},{4,20},{8,24},{12,28},{16,0},{20,4},{24,8},{28,12},{1,17},{... | collective-permute-start | bytes 221192 | tf_op jit(solution)/shard_map/ppermute | solution.py:152
  23.3 0.0 collective-permute-done.1.rest_2_.rest_1_
  23.3 1.9 %collective-permute-start.3 = (bf16[18,16,128]{2,1,0:T(8,128)(2,1)S(1)}, bf16[18,16,128]{2,1,0:T(8,128)(2,1)S(1)}, u32[]{:S(2)}, u32[]{:S(2)}) collective-permute-start(bf16[18,16,128]{2,1,0:T(8,128)(2,1)S(1)} %get-tuple-element.36), channel_id=1, source_target_pairs={{0,20},{4,16},{8,28},{12,24},{16,4},{20,0},{24,12},{28,8},{1,21},{... | collective-permute-start | bytes 221192 | tf_op jit(solution)/shard_map/ppermute | solution.py:152
  25.2 0.0 copy-done.4
  25.2 4.8 %permute_piece.5 = (bf16[18,16,128]{2,1,0:T(8,128)(2,1)S(1)}, bf16[18,16,128]{2,1,0:T(8,128)(2,1)S(1)}, bf16[18,16,128]{2,1,0:T(8,128)(2,1)S(1)}, bf16[18,16,128]{2,1,0:T(8,128)(2,1)S(1)}) custom-call(s32[1]{0:T(128)} %bitcast.1.region, bf16[16,16384]{1,0:T(8,128)(2,1)S(1)} %copy-done.4, s32[128,128]{1,0:T(8,128)S(1)} %bitcast.19, s32[128,128]{1,0:T(8,128)S(1)} %bitcast.16, ...), custom_call_target="tpu_custom_call" | custom-call | flops 2000000000 | bytes 1000000 | tf_op jit(solution)/shard_map/permute_piece/pallas_call | solution.py:132
  30.0 1.5 %collective-permute-done.2.rest_2_ = bf16[18,16,128]{2,1,0:T(8,128)(2,1)S(1)} collective-permute-done((bf16[18,16,128]{2,1,0:T(8,128)(2,1)S(1)}, bf16[18,16,128]{2,1,0:T(8,128)(2,1)S(1)}, u32[]{:S(2)}, u32[]{:S(2)}) %collective-permute-start.2) | collective-permute-done | bytes 73760 | tf_op jit(solution)/shard_map/ppermute | solution.py:152
  31.6 0.0 collective-permute-start.4
  31.6 0.9 %collective-permute-done.3.rest_3_ = bf16[18,16,128]{2,1,0:T(8,128)(2,1)S(1)} collective-permute-done((bf16[18,16,128]{2,1,0:T(8,128)(2,1)S(1)}, bf16[18,16,128]{2,1,0:T(8,128)(2,1)S(1)}, u32[]{:S(2)}, u32[]{:S(2)}) %collective-permute-start.3) | collective-permute-done | bytes 73760 | tf_op jit(solution)/shard_map/ppermute | solution.py:152
  32.5 0.7 collective-permute-start.5
  33.2 0.0 collective-permute-done.7.rest_10_.one
  33.2 1.9 %collective-permute-start.6 = (bf16[18,16,128]{2,1,0:T(8,128)(2,1)S(1)}, bf16[18,16,128]{2,1,0:T(8,128)(2,1)S(1)}, u32[]{:S(2)}, u32[]{:S(2)}) collective-permute-start(bf16[18,16,128]{2,1,0:T(8,128)(2,1)S(1)} %get-tuple-element.39), channel_id=1, source_target_pairs={{0,4},{4,0},{8,12},{12,8},{16,20},{20,16},{24,28},{28,24},{1,5},{5... | collective-permute-start | bytes 221192 | tf_op jit(solution)/shard_map/ppermute | solution.py:152
  35.1 0.1 pad_add_fusion.place_of
  35.2 0.0 copy-done.2
  35.2 1.2 %links.1 = (s32[2,64]{1,0:T(2,128)S(1)}, bf16[27,64,80]{2,1,0:T(8,128)(2,1)S(1)}) custom-call(s32[2]{0:T(128)S(1)} %pad_add_fusion.place_of, s32[26,64]{1,0:T(8,128)S(1)} %bitcast.13, bf16[18,16,128]{2,1,0:T(8,128)(2,1)S(1)} %get-tuple-element.35.rest_0_._), custom_call_target="tpu_custom_call" | custom-call | tf_op jit(solution)/shard_map/links/pallas_call | solution.py:634
  36.3 0.0 collective-permute-done.8.rest_11_.two
  36.4 0.0 collective-permute-done.9.rest_12_.three
  36.4 0.0 collective-permute-done.4.rest_4_
  36.4 1.4 %collective-permute-done.5.rest_5_ = bf16[18,16,128]{2,1,0:T(8,128)(2,1)S(1)} collective-permute-done((bf16[18,16,128]{2,1,0:T(8,128)(2,1)S(1)}, bf16[18,16,128]{2,1,0:T(8,128)(2,1)S(1)}, u32[]{:S(2)}, u32[]{:S(2)}) %collective-permute-start.5) | collective-permute-done | bytes 73760 | tf_op jit(solution)/shard_map/ppermute | solution.py:152
  37.8 0.5 collective-permute-done.6.rest_6_
  38.3 4.9 %far_voxels.1.rest_8_ = bf16[4,512,128]{2,1,0:T(8,128)(2,1)S(1)} custom-call(s32[1]{0:T(128)} %bitcast.chan, bf16[18,16,128]{2,1,0:T(8,128)(2,1)S(1)} %collective-permute-done.rest_1_.rest_0_, bf16[18,16,128]{2,1,0:T(8,128)(2,1)S(1)} %collective-permute-done.1.rest_2_.rest_1_, bf16[18,16,128]{2,1,0:T(8,128)(2,1)S(1)} %collective-permute-done.2.rest_2_, ...), custom_call_target="tpu_custom_call" | custom-call | flops 4000000000 | bytes 1200000 | tf_op jit(solution)/shard_map/far_voxels/pallas_call | solution.py:327
  43.2 1.6 %collective-permute-start.12 = (bf16[4,512,128]{2,1,0:T(8,128)(2,1)S(1)}, bf16[4,512,128]{2,1,0:T(8,128)(2,1)S(1)}, u32[]{:S(2)}, u32[]{:S(2)}) collective-permute-start(bf16[4,512,128]{2,1,0:T(8,128)(2,1)S(1)} %far_voxels.1.rest_8_), channel_id=1, source_target_pairs={{0,2},{1,3},{2,0},{3,1},{4,6},{5,7},{6,4},{7,5},{8,10},{9,11},{10,... | collective-permute-start | bytes 1572872 | tf_op jit(solution)/shard_map/ppermute | solution.py:658
  44.8 5.4 %near_voxels.1 = (bf16[2,512,128]{2,1,0:T(8,128)(2,1)S(1)}, bf16[4,512,128]{2,1,0:T(8,128)(2,1)S(1)}, bf16[4,512,128]{2,1,0:T(8,128)(2,1)S(1)}, bf16[8,16,128]{2...) custom-call(s32[1]{0:T(128)} %bitcast.chan, ...), custom_call_target="tpu_custom_call" | custom-call | flops 4000000000 | bytes 3000000 | tf_op jit(solution)/shard_map/near_voxels/pallas_call | solution.py:340
  50.2 3.7 %collective-permute-start.16 = (bf16[8,16,128]{2,1,0:T(8,128)(2,1)S(1)}, bf16[8,16,128]{2,1,0:T(8,128)(2,1)S(1)}, u32[]{:S(2)}, u32[]{:S(2)}) collective-permute-start(bf16[8,16,128]{2,1,0:T(8,128)(2,1)S(1)} %get-tuple-element.50), channel_id=1, source_target_pairs={{0,4},{4,8},{8,12},{12,16},{16,20},{20,24},{24,28},{7,3},{11,7},{1... | collective-permute-start | bytes 98312 | tf_op jit(solution)/shard_map/ppermute | solution.py:653
  53.8 0.7 collective-permute-start.17
  54.5 0.0 copy-start.5
  54.5 0.1 collective-permute-start.10
  54.6 1.5 %prepare.1 = (bf16[2,9,256,256]{3,2,1,0:T(8,128)(2,1)S(1)}, bf16[2,9,256,256]{3,2,1,0:T(8,128)(2,1)S(1)}, bf16[128,512]{1,0:T(8,128)(2,1)S(1)}) custom-call(s32[1]{0:T(128)} %bitcast.chan, bf16[17,16,192]{2,1,0:T(8,128)(2,1)S(1)} %pack.1.own, bf16[17,16,192]{2,1,0:T(8,128)(2,1)S(1)} %collective-permute-done.7.rest_10_.one, ...), custom_call_target="tpu_custom_call" | custom-call | flops 2000000000 | bytes 3000000 | tf_op jit(solution)/shard_map/prepare/pallas_call | solution.py:429
  56.1 4.1 %collective-permute-start.11 = (bf16[2,512,128]{2,1,0:T(8,128)(2,1)S(1)}, bf16[2,512,128]{2,1,0:T(8,128)(2,1)S(1)}, u32[]{:S(2)}, u32[]{:S(2)}) collective-permute-start(bf16[2,512,128]{2,1,0:T(8,128)(2,1)S(1)} %get-tuple-element.44), channel_id=1, source_target_pairs={{0,3},{1,2},{2,1},{3,0},{4,7},{5,6},{6,5},{7,4},{8,11},{9,10},{10,... | collective-permute-start | bytes 786440 | tf_op jit(solution)/shard_map/ppermute | solution.py:658
  60.2 0.0 collective-permute-done.12.planes.two
  60.2 0.7 collective-permute-start.14
  60.9 0.0 collective-permute-done.16.r0
  61.0 0.7 collective-permute-start.15
  61.6 0.0 collective-permute-done.17.r2
  61.6 2.0 %collective-permute-start.13 = (bf16[2,512,128]{2,1,0:T(8,128)(2,1)S(1)}, bf16[2,512,128]{2,1,0:T(8,128)(2,1)S(1)}, u32[]{:S(2)}, u32[]{:S(2)}) collective-permute-start(bf16[2,512,128]{2,1,0:T(8,128)(2,1)S(1)} %shared_planes.1), channel_id=1, source_target_pairs={{0,1},{1,0},{2,3},{3,2},{4,5},{5,4},{6,7},{7,6},{8,9},{9,8},{10,11... | collective-permute-start | bytes 786440 | tf_op jit(solution)/shard_map/ppermute | solution.py:658
  63.6 0.0 copy-done.5
  63.6 3.9 %even_sums.1.sums = f32[2,2,512,256]{3,2,1,0:T(8,128)S(1)} custom-call(bf16[4,512,128]{2,1,0:T(8,128)(2,1)S(1)} %get-tuple-element.49.own, bf16[4,512,128]{2,1,0:T(8,128)(2,1)S(1)} %collective-permute-done.12.planes.two, bf16[8,16,128]{2,1,0:T(8,128)(2,1)S(1)} %collective-permute-done.16.r0, bf16[8,16,128]{2,1,0:T(8,128)(2,1)S(1)} %collective-permute-done.17.r2, ...), custom_call_target="tpu_custom_call" | custom-call | flops 4000000000 | bytes 5000000 | tf_op jit(solution)/shard_map/even_sums/pallas_call | solution.py:536
  67.5 0.0 collective-permute-done.14.r1
  67.5 0.0 collective-permute-done.15.r3
  67.5 0.0 collective-permute-done.11.direct
  67.5 0.0 collective-permute-done.10.one
  67.5 0.0 collective-permute-done.13.passed
  67.5 4.3 %convolve.1 = (bf16[32,1024]{1,0:T(8,128)(2,1)S(1)}, bf16[32,1024]{1,0:T(8,128)(2,1)S(1)}, bf16[32,1024]{1,0:T(8,128)(2,1)S(1)}, bf16[32,1024]{1,0:T(8,128)(2,1)S(1)}) custom-call(s32[1]{0:T(128)} %bitcast.chan, s32[1]{0:T(128)S(6)} %copy.10.active, bf16[4,512,128]{2,1,0:T(8,128)(2,1)S(1)} %collective-permute-done.10.one, ...), custom_call_target="tpu_custom_call" | custom-call | flops 4000000000 | bytes 5000000 | tf_op jit(solution)/shard_map/convolve/pallas_call | solution.py:555
  71.8 0.1 collective-permute-start.18
  71.9 2.1 %collective-permute-start.19 = (bf16[32,1024]{1,0:T(8,128)(2,1)S(1)}, bf16[32,1024]{1,0:T(8,128)(2,1)S(1)}, u32[]{:S(2)}, u32[]{:S(2)}) collective-permute-start(bf16[32,1024]{1,0:T(8,128)(2,1)S(1)} %get-tuple-element.55), channel_id=1, source_target_pairs={{0,2},{1,3},{2,0},{3,1},{4,6},{5,7},{6,4},{7,5},{8,10},{9,11},{10,... | collective-permute-start | bytes 196616 | tf_op jit(solution)/shard_map/ppermute | solution.py:658
  74.1 0.1 collective-permute-start.20
  74.1 0.0 collective-permute-done.18.one
  74.2 2.6 %collective-permute-done.19.two = bf16[32,1024]{1,0:T(8,128)(2,1)S(1)} collective-permute-done((bf16[32,1024]{1,0:T(8,128)(2,1)S(1)}, bf16[32,1024]{1,0:T(8,128)(2,1)S(1)}, u32[]{:S(2)}, u32[]{:S(2)}) %collective-permute-start.19) | collective-permute-done | bytes 65568 | tf_op jit(solution)/shard_map/ppermute | solution.py:658
  76.8 1.4 %collective-permute-done.20.three = bf16[32,1024]{1,0:T(8,128)(2,1)S(1)} collective-permute-done((bf16[32,1024]{1,0:T(8,128)(2,1)S(1)}, bf16[32,1024]{1,0:T(8,128)(2,1)S(1)}, u32[]{:S(2)}, u32[]{:S(2)}) %collective-permute-start.20) | collective-permute-done | bytes 65568 | tf_op jit(solution)/shard_map/ppermute | solution.py:658
  78.1 1.9 %finish.1 = bf16[64,2048]{1,0:T(8,128)(2,1)} custom-call(s32[1]{0:T(128)} %bitcast.chan, bf16[32,1024]{1,0:T(8,128)(2,1)S(1)} %get-tuple-element.53.own, bf16[32,1024]{1,0:T(8,128)(2,1)S(1)} %collective-permute-done.18.one, bf16[32,1024]{1,0:T(8,128)(2,1)S(1)} %collective-permute-done.19.two, bf16[32,1024]{1,0:T(8,128)(2,1)S(1)} %collective-permute-done.20.three), custom_call_target="tpu_custom_call" | custom-call | tf_op jit(solution)/shard_map/finish/pallas_call | solution.py:586
  (6 shorter events, 0.0 us)
Async XLA Ops:
  7.5 1.0 %copy-start.3 = (bf16[16,16384]{1,0:T(8,128)(2,1)S(1)}, bf16[16,16384]{1,0:T(8,128)(2,1)}, u32[]{:S(2)}) copy-start(bf16[16,16384]{1,0:T(8,128)(2,1)} %feats.5) | copy-start | bytes 1572868
  11.0 11.4 %collective-permute-start = (bf16[18,16,128]{2,1,0:T(8,128)(2,1)S(1)}, bf16[18,16,128]{2,1,0:T(8,128)(2,1)S(1)}, u32[]{:S(2)}, u32[]{:S(2)}) collective-permute-start(bf16[18,16,128]{2,1,0:T(8,128)(2,1)S(1)} %get-tuple-element.33.rest_0_), channel_id=1, source_target_pairs={{0,24},{4,28},{8,16},{12,20},{16,8},{20,12},{24,0},{28,4},{1,25},{... | collective-permute-start | bytes 221192 | tf_op jit(solution)/shard_map/ppermute | solution.py:152
  16.1 3.6 %copy-start = (bf16[16,64,3,3,3]{1,0,4,3,2:T(8,128)(2,1)S(1)}, bf16[16,64,3,3,3]{1,0,4,3,2:T(8,128)(2,1)}, u32[]{:S(2)}) copy-start(bf16[16,64,3,3,3]{1,0,4,3,2:T(8,128)(2,1)} %param.14) | copy-start | bytes 165892
  16.1 3.6 %copy-start.1 = (bf16[128,16,2,2,2]{0,4,3,2,1:T(2,128)(2,1)S(1)}, bf16[128,16,2,2,2]{0,4,3,2,1:T(2,128)(2,1)}, u32[]{:S(2)}) copy-start(bf16[128,16,2,2,2]{0,4,3,2,1:T(2,128)(2,1)} %param.15) | copy-start | bytes 98308
  16.1 9.2 %copy-start.4 = (bf16[16,16384]{1,0:T(8,128)(2,1)S(1)}, bf16[16,16384]{1,0:T(8,128)(2,1)}, u32[]{:S(2)}) copy-start(bf16[16,16384]{1,0:T(8,128)(2,1)} %feats.5) | copy-start | bytes 1572868
  16.1 7.3 %collective-permute-start.1 = (bf16[18,16,128]{2,1,0:T(8,128)(2,1)S(1)}, bf16[18,16,128]{2,1,0:T(8,128)(2,1)S(1)}, u32[]{:S(2)}, u32[]{:S(2)}) collective-permute-start(bf16[18,16,128]{2,1,0:T(8,128)(2,1)S(1)} %get-tuple-element.34), channel_id=1, source_target_pairs={{0,28},{4,24},{8,20},{12,16},{16,12},{20,8},{24,4},{28,0},{1,29},{... | collective-permute-start | bytes 221192 | tf_op jit(solution)/shard_map/ppermute | solution.py:152
  19.8 13.4 %collective-permute-start.7 = (bf16[17,16,192]{2,1,0:T(8,128)(2,1)S(1)}, bf16[17,16,192]{2,1,0:T(8,128)(2,1)S(1)}, u32[]{:S(2)}, u32[]{:S(2)}) collective-permute-start(bf16[17,16,192]{2,1,0:T(8,128)(2,1)S(1)} %pack.1.own), channel_id=1, source_target_pairs={{0,1},{1,0},{2,3},{3,2},{4,5},{5,4},{6,7},{7,6},{8,9},{9,8},{10,11... | collective-permute-start | bytes 313352 | tf_op jit(solution)/shard_map/ppermute | solution.py:658
  19.8 16.5 %collective-permute-start.8 = (bf16[17,16,192]{2,1,0:T(8,128)(2,1)S(1)}, bf16[17,16,192]{2,1,0:T(8,128)(2,1)S(1)}, u32[]{:S(2)}, u32[]{:S(2)}) collective-permute-start(bf16[17,16,192]{2,1,0:T(8,128)(2,1)S(1)} %pack.1.own), channel_id=1, source_target_pairs={{0,2},{1,3},{2,0},{3,1},{4,6},{5,7},{6,4},{7,5},{8,10},{9,11},{10,... | collective-permute-start | bytes 313352 | tf_op jit(solution)/shard_map/ppermute | solution.py:658
  21.4 14.9 %collective-permute-start.9 = (bf16[17,16,192]{2,1,0:T(8,128)(2,1)S(1)}, bf16[17,16,192]{2,1,0:T(8,128)(2,1)S(1)}, u32[]{:S(2)}, u32[]{:S(2)}) collective-permute-start(bf16[17,16,192]{2,1,0:T(8,128)(2,1)S(1)} %pack.1.own), channel_id=1, source_target_pairs={{0,3},{1,2},{2,1},{3,0},{4,7},{5,6},{6,5},{7,4},{8,11},{9,10},{10,... | collective-permute-start | bytes 313352 | tf_op jit(solution)/shard_map/ppermute | solution.py:658
  22.4 9.2 %collective-permute-start.2 = (bf16[18,16,128]{2,1,0:T(8,128)(2,1)S(1)}, bf16[18,16,128]{2,1,0:T(8,128)(2,1)S(1)}, u32[]{:S(2)}, u32[]{:S(2)}) collective-permute-start(bf16[18,16,128]{2,1,0:T(8,128)(2,1)S(1)} %get-tuple-element.35.rest_0_._), channel_id=1, source_target_pairs={{0,16},{4,20},{8,24},{12,28},{16,0},{20,4},{24,8},{28,12},{1,17},{... | collective-permute-start | bytes 221192 | tf_op jit(solution)/shard_map/ppermute | solution.py:152
  23.3 11.8 %copy-start.2 = (s32[64,26]{0,1:T(8,128)S(1)}, s32[64,26]{0,1:T(8,128)}, u32[]{:S(2)}) copy-start(s32[64,26]{0,1:T(8,128)} %param.12) | copy-start | bytes 19972
  23.3 9.1 %collective-permute-start.3 = (bf16[18,16,128]{2,1,0:T(8,128)(2,1)S(1)}, bf16[18,16,128]{2,1,0:T(8,128)(2,1)S(1)}, u32[]{:S(2)}, u32[]{:S(2)}) collective-permute-start(bf16[18,16,128]{2,1,0:T(8,128)(2,1)S(1)} %get-tuple-element.36), channel_id=1, source_target_pairs={{0,20},{4,16},{8,28},{12,24},{16,4},{20,0},{24,12},{28,8},{1,21},{... | collective-permute-start | bytes 221192 | tf_op jit(solution)/shard_map/ppermute | solution.py:152
  31.6 4.8 %collective-permute-start.4 = (bf16[18,16,128]{2,1,0:T(8,128)(2,1)S(1)}, bf16[18,16,128]{2,1,0:T(8,128)(2,1)S(1)}, u32[]{:S(2)}, u32[]{:S(2)}) collective-permute-start(bf16[18,16,128]{2,1,0:T(8,128)(2,1)S(1)} %get-tuple-element.37), channel_id=1, source_target_pairs={{0,8},{4,12},{8,0},{12,4},{16,24},{20,28},{24,16},{28,20},{1,9},{5... | collective-permute-start | bytes 221192 | tf_op jit(solution)/shard_map/ppermute | solution.py:152
  32.5 5.4 %collective-permute-start.5 = (bf16[18,16,128]{2,1,0:T(8,128)(2,1)S(1)}, bf16[18,16,128]{2,1,0:T(8,128)(2,1)S(1)}, u32[]{:S(2)}, u32[]{:S(2)}) collective-permute-start(bf16[18,16,128]{2,1,0:T(8,128)(2,1)S(1)} %get-tuple-element.38), channel_id=1, source_target_pairs={{0,12},{4,8},{8,4},{12,0},{16,28},{20,24},{24,20},{28,16},{1,13},{... | collective-permute-start | bytes 221192 | tf_op jit(solution)/shard_map/ppermute | solution.py:152
  33.2 5.1 %collective-permute-start.6 = (bf16[18,16,128]{2,1,0:T(8,128)(2,1)S(1)}, bf16[18,16,128]{2,1,0:T(8,128)(2,1)S(1)}, u32[]{:S(2)}, u32[]{:S(2)}) collective-permute-start(bf16[18,16,128]{2,1,0:T(8,128)(2,1)S(1)} %get-tuple-element.39), channel_id=1, source_target_pairs={{0,4},{4,0},{8,12},{12,8},{16,20},{20,16},{24,28},{28,24},{1,5},{5... | collective-permute-start | bytes 221192 | tf_op jit(solution)/shard_map/ppermute | solution.py:152
  43.2 17.0 %collective-permute-start.12 = (bf16[4,512,128]{2,1,0:T(8,128)(2,1)S(1)}, bf16[4,512,128]{2,1,0:T(8,128)(2,1)S(1)}, u32[]{:S(2)}, u32[]{:S(2)}) collective-permute-start(bf16[4,512,128]{2,1,0:T(8,128)(2,1)S(1)} %far_voxels.1.rest_8_), channel_id=1, source_target_pairs={{0,2},{1,3},{2,0},{3,1},{4,6},{5,7},{6,4},{7,5},{8,10},{9,11},{10,... | collective-permute-start | bytes 1572872 | tf_op jit(solution)/shard_map/ppermute | solution.py:658
  50.2 10.8 %collective-permute-start.16 = (bf16[8,16,128]{2,1,0:T(8,128)(2,1)S(1)}, bf16[8,16,128]{2,1,0:T(8,128)(2,1)S(1)}, u32[]{:S(2)}, u32[]{:S(2)}) collective-permute-start(bf16[8,16,128]{2,1,0:T(8,128)(2,1)S(1)} %get-tuple-element.50), channel_id=1, source_target_pairs={{0,4},{4,8},{8,12},{12,16},{16,20},{20,24},{24,28},{7,3},{11,7},{1... | collective-permute-start | bytes 98312 | tf_op jit(solution)/shard_map/ppermute | solution.py:653
  53.8 7.8 %collective-permute-start.17 = (bf16[8,16,128]{2,1,0:T(8,128)(2,1)S(1)}, bf16[8,16,128]{2,1,0:T(8,128)(2,1)S(1)}, u32[]{:S(2)}, u32[]{:S(2)}) collective-permute-start(bf16[8,16,128]{2,1,0:T(8,128)(2,1)S(1)} %get-tuple-element.51), channel_id=1, source_target_pairs={{2,4},{6,8},{10,12},{14,16},{18,20},{22,24},{26,28},{5,3},{9,7},{1... | collective-permute-start | bytes 98312 | tf_op jit(solution)/shard_map/ppermute | solution.py:653
  54.5 9.1 %copy-start.5 = (bf16[256,128]{1,0:T(8,128)(2,1)S(1)}, bf16[256,128]{1,0:T(8,128)(2,1)}, u32[]{:S(2)}) copy-start(bf16[256,128]{1,0:T(8,128)(2,1)} %constant.64.clone.pick) | copy-start | bytes 196612
  54.5 13.0 %collective-permute-start.10 = (bf16[4,512,128]{2,1,0:T(8,128)(2,1)S(1)}, bf16[4,512,128]{2,1,0:T(8,128)(2,1)S(1)}, u32[]{:S(2)}, u32[]{:S(2)}) collective-permute-start(bf16[4,512,128]{2,1,0:T(8,128)(2,1)S(1)} %get-tuple-element.43), channel_id=1, source_target_pairs={{0,1},{1,0},{2,3},{3,2},{4,5},{5,4},{6,7},{7,6},{8,9},{9,8},{10,11... | collective-permute-start | bytes 1572872 | tf_op jit(solution)/shard_map/ppermute | solution.py:658
  56.1 11.4 %collective-permute-start.11 = (bf16[2,512,128]{2,1,0:T(8,128)(2,1)S(1)}, bf16[2,512,128]{2,1,0:T(8,128)(2,1)S(1)}, u32[]{:S(2)}, u32[]{:S(2)}) collective-permute-start(bf16[2,512,128]{2,1,0:T(8,128)(2,1)S(1)} %get-tuple-element.44), channel_id=1, source_target_pairs={{0,3},{1,2},{2,1},{3,0},{4,7},{5,6},{6,5},{7,4},{8,11},{9,10},{10,... | collective-permute-start | bytes 786440 | tf_op jit(solution)/shard_map/ppermute | solution.py:658
  60.2 7.2 %collective-permute-start.14 = (bf16[8,16,128]{2,1,0:T(8,128)(2,1)S(1)}, bf16[8,16,128]{2,1,0:T(8,128)(2,1)S(1)}, u32[]{:S(2)}, u32[]{:S(2)}) collective-permute-start(bf16[8,16,128]{2,1,0:T(8,128)(2,1)S(1)} %get-tuple-element.45), channel_id=1, source_target_pairs={{1,4},{5,8},{9,12},{13,16},{17,20},{21,24},{25,28},{6,3},{10,7},{1... | collective-permute-start | bytes 98312 | tf_op jit(solution)/shard_map/ppermute | solution.py:653
  61.0 6.6 %collective-permute-start.15 = (bf16[8,16,128]{2,1,0:T(8,128)(2,1)S(1)}, bf16[8,16,128]{2,1,0:T(8,128)(2,1)S(1)}, u32[]{:S(2)}, u32[]{:S(2)}) collective-permute-start(bf16[8,16,128]{2,1,0:T(8,128)(2,1)S(1)} %get-tuple-element.46), channel_id=1, source_target_pairs={{3,4},{7,8},{11,12},{15,16},{19,20},{23,24},{27,28},{4,3},{8,7},{1... | collective-permute-start | bytes 98312 | tf_op jit(solution)/shard_map/ppermute | solution.py:653
  61.6 5.9 %collective-permute-start.13 = (bf16[2,512,128]{2,1,0:T(8,128)(2,1)S(1)}, bf16[2,512,128]{2,1,0:T(8,128)(2,1)S(1)}, u32[]{:S(2)}, u32[]{:S(2)}) collective-permute-start(bf16[2,512,128]{2,1,0:T(8,128)(2,1)S(1)} %shared_planes.1), channel_id=1, source_target_pairs={{0,1},{1,0},{2,3},{3,2},{4,5},{5,4},{6,7},{7,6},{8,9},{9,8},{10,11... | collective-permute-start | bytes 786440 | tf_op jit(solution)/shard_map/ppermute | solution.py:658
  71.8 2.3 %collective-permute-start.18 = (bf16[32,1024]{1,0:T(8,128)(2,1)S(1)}, bf16[32,1024]{1,0:T(8,128)(2,1)S(1)}, u32[]{:S(2)}, u32[]{:S(2)}) collective-permute-start(bf16[32,1024]{1,0:T(8,128)(2,1)S(1)} %get-tuple-element.54), channel_id=1, source_target_pairs={{0,1},{1,0},{2,3},{3,2},{4,5},{5,4},{6,7},{7,6},{8,9},{9,8},{10,11... | collective-permute-start | bytes 196616 | tf_op jit(solution)/shard_map/ppermute | solution.py:658
  71.9 4.8 %collective-permute-start.19 = (bf16[32,1024]{1,0:T(8,128)(2,1)S(1)}, bf16[32,1024]{1,0:T(8,128)(2,1)S(1)}, u32[]{:S(2)}, u32[]{:S(2)}) collective-permute-start(bf16[32,1024]{1,0:T(8,128)(2,1)S(1)} %get-tuple-element.55), channel_id=1, source_target_pairs={{0,2},{1,3},{2,0},{3,1},{4,6},{5,7},{6,4},{7,5},{8,10},{9,11},{10,... | collective-permute-start | bytes 196616 | tf_op jit(solution)/shard_map/ppermute | solution.py:658
  74.1 4.0 %collective-permute-start.20 = (bf16[32,1024]{1,0:T(8,128)(2,1)S(1)}, bf16[32,1024]{1,0:T(8,128)(2,1)S(1)}, u32[]{:S(2)}, u32[]{:S(2)}) collective-permute-start(bf16[32,1024]{1,0:T(8,128)(2,1)S(1)} %get-tuple-element.56), channel_id=1, source_target_pairs={{0,3},{1,2},{2,1},{3,0},{4,7},{5,6},{6,5},{7,4},{8,11},{9,10},{10,... | collective-permute-start | bytes 196616 | tf_op jit(solution)/shard_map/ppermute | solution.py:658
